TPU v7x, 256 devices: a whole 4x4x8 slice. The times are simulated.
256 devices in a mesh: section: 8 (over y, z_hi), dp: 32 (over z_lo, x, core).
Axes of the slice: x: 4, y: 4, z: 8 (z_hi: 2, z_lo: 4; z = z_hi * 4 + z_lo), core: 2. Of those that a mesh axis runs over, the one named last changes fastest.
Arguments:
- inputs: bfloat16 [32, 8, 16, 7168], P('dp')
- cotangent: bfloat16 [32, 8, 16, 7168], P('dp'), may hold values from -0.09375 to 0.09375
- send_memory: bfloat16 [8, 32, 8, 16, 7168], P('section', 'dp')
- recv_memory: bfloat16 [8, 32, 8, 16, 7168], P('section', 'dp')
- sample_ids: int32 [32, 8], P('dp'), may hold values from 0 to 7, each once within a row
- gains: bfloat16 [8, 2, 7168], P('section'), may hold values from 0.099609375 to 1.8984375
- down_weight: bfloat16 [8, 2, 7168, 64], P('section'), may hold values from -0.0625 to 0.0625
- up_weight: bfloat16 [8, 2, 64, 7168], P('section'), may hold values from -0.75 to 0.75
Outputs:
- grad_down: bfloat16 [8, 2, 7168, 64], P('section', None, 'dp')
- grad_up: bfloat16 [8, 2, 64, 7168], P('section', None, None, 'dp')
- grad_gain: bfloat16 [8, 2, 7168], P('section', None, 'dp')
Inputs may be any that keep to these rules, and one draw needn't show every extreme that they name: `sample_ids`: each row names every slot 0 to 7 once.
All inputs are finite; a program needn't handle non-finite values.
Results may differ from a plain program's by a relative error of at most 0.035.
Values may be sent and summed in bfloat16 or wider, within the bound.
A program may use at most 128 MiB of HBM per device.

v0:
```python
import jax
import jax.numpy as jnp
from jax import lax
from jax.sharding import PartitionSpec as P

EPSILON = 1e-05
SQUARE_EPS = 1e-06
CLIP_RANGE = 2.0


def from_behind(block, axis, distance):
    devices = range(lax.axis_size(axis))
    route = [(i - distance, i) for i in devices if i - distance in devices]
    return lax.ppermute(block, axis, route)


def section_map(stream, gain_rows, down_rows, up_rows):
    for layer_no in range(down_rows.shape[0]):
        widened = stream.astype(jnp.float32)
        average = jnp.mean(widened, axis=-1, keepdims=True)
        centred = widened - average
        spread = jnp.mean(centred * centred, axis=-1, keepdims=True)
        normed = (
            centred * lax.rsqrt(spread + EPSILON) * gain_rows[layer_no].astype(jnp.float32)
        ).astype(jnp.bfloat16)
        hidden = jax.nn.gelu(
            jnp.dot(normed, down_rows[layer_no], preferred_element_type=jnp.float32),
            approximate=True,
        ).astype(jnp.bfloat16)
        branch = jnp.dot(hidden, up_rows[layer_no], preferred_element_type=jnp.float32)
        stream = (widened + branch).astype(jnp.bfloat16)
    return stream


def block_scale(values):
    blocked = values.reshape(values.shape[:-1] + (values.shape[-1] // 128, 128))
    factor = (CLIP_RANGE * jnp.sqrt(jnp.mean(blocked * blocked, axis=-1) + SQUARE_EPS)).astype(
        jnp.bfloat16
    )
    factor = lax.optimization_barrier(factor)
    symbols = jnp.clip(blocked / factor.astype(jnp.float32)[..., None], -1.0, 1.0).astype(
        jnp.bfloat16
    )
    symbols, factor = lax.optimization_barrier((symbols.reshape(values.shape), factor))
    return (symbols, factor)


def block_value(symbols, factor):
    blocked = symbols.astype(jnp.float32).reshape(factor.shape + (128,))
    return (blocked * factor.astype(jnp.float32)[..., None]).reshape(symbols.shape)


def pull_section(stream, gain_rows, down_rows, up_rows, incoming):
    result_now, pullback = jax.vjp(section_map, stream, gain_rows, down_rows, up_rows)
    return pullback(incoming)


def local(inputs, cotangent, send_memory, recv_memory, sample_ids, gains, down_weight, up_weight):
    sections = lax.axis_size("section")
    section_at = lax.axis_index("section")
    section_inputs = inputs[0]
    last_grads = cotangent[0]
    sent_table = send_memory[0, 0]
    kept_table = recv_memory[0, 0]
    sample_order = sample_ids[0]
    gain_rows = gains[0]
    down_rows = down_weight[0]
    up_rows = up_weight[0]
    micro_count, seq_len, feature_count = section_inputs.shape
    block_count = feature_count // 128
    tick_count = micro_count + sections - 1
    empty_symbols = jnp.zeros((seq_len, feature_count), jnp.bfloat16)
    empty_factor = jnp.zeros((seq_len, block_count), jnp.bfloat16)

    def forward_tick(state_now, moment):
        symbols, factor, stash_rows = state_now
        micro_no = moment - section_at
        usable = jnp.logical_and(micro_no >= 0, micro_no < micro_count)
        position = jnp.clip(micro_no, 0, micro_count - 1)
        slot_no = sample_order[position]
        kept_base = lax.dynamic_index_in_dim(kept_table, slot_no, 0, keepdims=False)
        rebuilt = (kept_base.astype(jnp.float32) + block_value(symbols, factor)).astype(
            jnp.bfloat16
        )
        first_in = lax.dynamic_index_in_dim(section_inputs, position, 0, keepdims=False)
        stream = jnp.where(section_at == 0, first_in, rebuilt)
        current = lax.dynamic_index_in_dim(stash_rows, position, 0, keepdims=False)
        stash_rows = lax.dynamic_update_index_in_dim(
            stash_rows, jnp.where(usable, stream, current), position, 0
        )
        output = section_map(stream, gain_rows, down_rows, up_rows)
        sent_base = lax.dynamic_index_in_dim(sent_table, slot_no, 0, keepdims=False)
        out_symbols, out_factor = block_scale(
            output.astype(jnp.float32) - sent_base.astype(jnp.float32)
        )
        symbols, factor = from_behind((out_symbols, out_factor), "section", 1)
        return ((symbols, factor, stash_rows), None)

    start_stash = jnp.zeros(section_inputs.shape, jnp.bfloat16)
    forward_state, unused_out = lax.scan(
        forward_tick, (empty_symbols, empty_factor, start_stash), jnp.arange(tick_count)
    )
    stash_rows = forward_state[2]

    def backward_tick(state_now, moment):
        symbols, factor, running = state_now
        micro_no = moment - (sections - 1 - section_at)
        usable = jnp.logical_and(micro_no >= 0, micro_no < micro_count)
        position = jnp.clip(micro_no, 0, micro_count - 1)
        arrived = block_value(symbols, factor).astype(jnp.bfloat16)
        first_in = lax.dynamic_index_in_dim(last_grads, position, 0, keepdims=False)
        incoming = jnp.where(section_at == sections - 1, first_in, arrived)
        stream = lax.dynamic_index_in_dim(stash_rows, position, 0, keepdims=False)
        back_grad, grad_g, grad_d, grad_u = pull_section(
            stream, gain_rows, down_rows, up_rows, incoming
        )
        running = (
            running[0] + jnp.where(usable, grad_d.astype(jnp.float32), 0.0),
            running[1] + jnp.where(usable, grad_u.astype(jnp.float32), 0.0),
            running[2] + jnp.where(usable, grad_g.astype(jnp.float32), 0.0),
        )
        out_symbols, out_factor = block_scale(back_grad.astype(jnp.float32))
        symbols, factor = from_behind((out_symbols, out_factor), "section", -1)
        return ((symbols, factor, running), None)

    start_sums = (
        jnp.zeros(down_rows.shape, jnp.float32),
        jnp.zeros(up_rows.shape, jnp.float32),
        jnp.zeros(gain_rows.shape, jnp.float32),
    )
    backward_state, unused_back = lax.scan(
        backward_tick, (empty_symbols, empty_factor, start_sums), jnp.arange(tick_count)
    )
    local_sums = backward_state[2]
    summed = (
        lax.psum(local_sums[0].astype(jnp.bfloat16), "dp").astype(jnp.float32),
        lax.psum(local_sums[1].astype(jnp.bfloat16), "dp").astype(jnp.float32),
        lax.psum(local_sums[2].astype(jnp.bfloat16), "dp").astype(jnp.float32),
    )
    share = feature_count // lax.axis_size("dp")
    start_at = lax.axis_index("dp") * share
    pieces = (
        lax.dynamic_slice_in_dim(summed[0], start_at, share, 1),
        lax.dynamic_slice_in_dim(summed[1], start_at, share, 2),
        lax.dynamic_slice_in_dim(summed[2], start_at, share, 1),
    )
    return (
        pieces[0].astype(jnp.bfloat16)[None],
        pieces[1].astype(jnp.bfloat16)[None],
        pieces[2].astype(jnp.bfloat16)[None],
    )


def solution(mesh):
    in_specs = (
        P("dp", None, None, None),
        P("dp", None, None, None),
        P("section", "dp", None, None, None),
        P("section", "dp", None, None, None),
        P("dp", None),
        P("section", None, None),
        P("section", None, None, None),
        P("section", None, None, None),
    )
    out_specs = (
        P("section", None, "dp", None),
        P("section", None, None, "dp"),
        P("section", None, "dp"),
    )
    return jax.shard_map(local, mesh=mesh, in_specs=in_specs, out_specs=out_specs, check_vma=False)
```

profile of v0, /device:TPU:4, one launch (start us, length us, event | category | flops | bytes accessed | tf_op | source)
XLA Modules:
  0.0 1359.6 jit_solution(3743799652091846112)
XLA Ops:
  7.2 4.6 copy.11
  14.0 434.0 %while.37 = (s32[]{:T(128)}, bf16[16,7168]{1,0:T(8,128)(2,1)S(1)}, bf16[16,56]{1,0:T(8,128)(2,1)S(1)}, bf16[8,16,7168]{2,1,0:T(8,128)(2,1)}, pred[]{:T(512)}, /*...) while((s32[]{:T(128)}, bf16[16,7168]{1,0:T(8,128)(2,1)S(1)}, ...), condition=%wide.region_6.7_spmd, body=%wide.region_0.6_spmd.sunk | while | flops 63343272 | bytes 16681989 | solution.py:100
  27.0 9.1 collective-permute-start
  38.1 8.0 collective-permute-done.1
  59.2 8.3 collective-permute-start
  70.7 4.1 collective-permute-done.1
  87.8 8.3 collective-permute-start
  96.1 5.6 collective-permute-start.1
  116.2 8.3 collective-permute-start
  124.6 5.7 collective-permute-start.1
  144.8 8.4 collective-permute-start
  153.1 6.1 collective-permute-start.1
  173.6 8.1 collective-permute-start
  181.7 6.0 collective-permute-start.1
  202.6 8.3 collective-permute-start
  210.9 5.2 collective-permute-start.1
  230.5 8.1 collective-permute-start
  238.6 6.0 collective-permute-start.1
  259.0 8.1 collective-permute-start
  267.1 5.6 collective-permute-start.1
  287.1 8.2 collective-permute-start
  295.3 7.0 collective-permute-start.1
  316.7 8.1 collective-permute-start
  324.8 7.3 collective-permute-start.1
  346.4 8.1 collective-permute-start
  354.5 7.4 collective-permute-start.1
  376.3 8.2 collective-permute-start
  402.3 8.2 collective-permute-start
  410.5 6.2 collective-permute-start.1
  431.1 8.2 collective-permute-start
  439.3 7.3 collective-permute-start.1
  449.8 587.9 %while.38 = (s32[]{:T(128)}, bf16[16,7168]{1,0:T(8,128)(2,1)}, bf16[16,56]{1,0:T(8,128)(2,1)}, f32[2,7168,64]{1,2,0:T(8,128)}, f32[2,64,7168]{2,1,0:T(8,128)}, /...) while((s32[]{:T(128)}, bf16[16,7168]{1,0:T(8,128)(2,1)}, ...), condition=%wide.region_19.20_spmd.clone, body=%wide.region_7.19_spmd.clone.sunk | while | flops 181268320 | bytes 64486572 | solution.py:131
  478.3 3.7 select_add_fusion.6
  513.8 4.8 select_add_fusion.6
  518.6 4.5 select_add_fusion.7
  552.4 4.8 select_add_fusion.6
  557.2 4.5 select_add_fusion.7
  591.0 4.8 select_add_fusion.6
  595.8 4.5 select_add_fusion.7
  629.6 4.8 select_add_fusion.6
  634.4 4.5 select_add_fusion.7
  668.6 4.8 select_add_fusion.6
  673.4 4.5 select_add_fusion.7
  708.5 4.8 select_add_fusion.6
  713.3 4.5 select_add_fusion.7
  748.3 4.8 select_add_fusion.6
  753.1 4.5 select_add_fusion.7
  788.2 4.8 select_add_fusion.6
  793.0 4.5 select_add_fusion.7
  828.0 4.8 select_add_fusion.6
  832.8 4.5 select_add_fusion.7
  867.9 4.8 select_add_fusion.6
  872.7 4.5 select_add_fusion.7
  907.7 4.8 select_add_fusion.6
  912.5 4.5 select_add_fusion.7
  947.6 4.8 select_add_fusion.6
  952.4 4.5 select_add_fusion.7
  987.4 4.8 select_add_fusion.6
  992.2 4.5 select_add_fusion.7
  1027.3 4.8 select_add_fusion.6
  1032.1 4.5 select_add_fusion.7
  1037.7 3.5 convert_element_type.403
  1045.5 122.1 %psum.23 = bf16[2,7168]{1,0:T(2,128)(2,1)S(1)} all-reduce(bf16[2,7168]{1,0:T(2,128)(2,1)S(1)} %convert_element_type.409), channel_id=1, replica_groups=mesh['section'=8,'dp'=32] {'dp'}, use_global_device_ids=true, to_apply=%region_22.23 | all-reduce | flops 14336 | bytes 57344 | tf_op jit(solution)/shard_map/psum | solution.py:138
  1168.2 181.3 %all-reduce.9.cloned.1.call-done = (bf16[2,7168,64]{1,2,0:T(8,128)(2,1)}, bf16[2,64,7168]{2,1,0:T(8,128)(2,1)}) async-done(((bf16[2,7168,64]{1,2,0:T(8,128)(2,1)}, bf16[2,64,7168]{2,1,0:T(8,128)(2,1)}), (bf16[2,7168,64]{1,2,0:T(8,128)(2,1)}, bf16[2,64,7168]{2,1,0:T(8,128)(2,1)})) %all-reduce.9.cloned.1.call-update) | async-done | bytes 3670032 | tf_op jit(solution)/shard_map/psum | solution.py:136
  (1482 shorter events, 631.3 us)
Async XLA Ops:
  7.2 1342.4 %all-reduce.9.cloned.1.call-start = ((), (), s32[]{:S(2)}) async-start(), calls=%async_computation | async-start | bytes 7340032 | tf_op jit(solution)/shard_map/psum | solution.py:136
  27.0 19.1 %collective-permute-start = (bf16[16,7168]{1,0:T(8,128)(2,1)S(1)}, bf16[16,7168]{1,0:T(8,128)(2,1)S(1)}, u32[]{:S(2)}, u32[]{:S(2)}) collective-permute-start(bf16[16,7168]{1,0:T(8,128)(2,1)S(1)} %fusion.233), channel_id=1, source_target_pairs={{0,32},{32,64},{64,96},{96,128},{128,160},{160,192},{192,224},{1,3... | collective-permute-start | bytes 688136 | tf_op jit(solution)/shard_map/while/body/eval_jaxpr/ppermute | solution.py:14
  36.2 10.0 collective-permute-start.1
  59.2 15.6 %collective-permute-start = (bf16[16,7168]{1,0:T(8,128)(2,1)S(1)}, bf16[16,7168]{1,0:T(8,128)(2,1)S(1)}, u32[]{:S(2)}, u32[]{:S(2)}) collective-permute-start(bf16[16,7168]{1,0:T(8,128)(2,1)S(1)} %fusion.233), channel_id=1, source_target_pairs={{0,32},{32,64},{64,96},{96,128},{128,160},{160,192},{192,224},{1,3... | collective-permute-start | bytes 688136 | tf_op jit(solution)/shard_map/while/body/eval_jaxpr/ppermute | solution.py:14
  67.5 7.3 collective-permute-start.1
  87.8 15.3 %collective-permute-start = (bf16[16,7168]{1,0:T(8,128)(2,1)S(1)}, bf16[16,7168]{1,0:T(8,128)(2,1)S(1)}, u32[]{:S(2)}, u32[]{:S(2)}) collective-permute-start(bf16[16,7168]{1,0:T(8,128)(2,1)S(1)} %fusion.233), channel_id=1, source_target_pairs={{0,32},{32,64},{64,96},{96,128},{128,160},{160,192},{192,224},{1,3... | collective-permute-start | bytes 688136 | tf_op jit(solution)/shard_map/while/body/eval_jaxpr/ppermute | solution.py:14
  96.1 7.0 collective-permute-start.1
  116.2 15.5 %collective-permute-start = (bf16[16,7168]{1,0:T(8,128)(2,1)S(1)}, bf16[16,7168]{1,0:T(8,128)(2,1)S(1)}, u32[]{:S(2)}, u32[]{:S(2)}) collective-permute-start(bf16[16,7168]{1,0:T(8,128)(2,1)S(1)} %fusion.233), channel_id=1, source_target_pairs={{0,32},{32,64},{64,96},{96,128},{128,160},{160,192},{192,224},{1,3... | collective-permute-start | bytes 688136 | tf_op jit(solution)/shard_map/while/body/eval_jaxpr/ppermute | solution.py:14
  124.6 7.2 collective-permute-start.1
  144.8 15.8 %collective-permute-start = (bf16[16,7168]{1,0:T(8,128)(2,1)S(1)}, bf16[16,7168]{1,0:T(8,128)(2,1)S(1)}, u32[]{:S(2)}, u32[]{:S(2)}) collective-permute-start(bf16[16,7168]{1,0:T(8,128)(2,1)S(1)} %fusion.233), channel_id=1, source_target_pairs={{0,32},{32,64},{64,96},{96,128},{128,160},{160,192},{192,224},{1,3... | collective-permute-start | bytes 688136 | tf_op jit(solution)/shard_map/while/body/eval_jaxpr/ppermute | solution.py:14
  153.1 7.4 collective-permute-start.1
  173.6 16.0 %collective-permute-start = (bf16[16,7168]{1,0:T(8,128)(2,1)S(1)}, bf16[16,7168]{1,0:T(8,128)(2,1)S(1)}, u32[]{:S(2)}, u32[]{:S(2)}) collective-permute-start(bf16[16,7168]{1,0:T(8,128)(2,1)S(1)} %fusion.233), channel_id=1, source_target_pairs={{0,32},{32,64},{64,96},{96,128},{128,160},{160,192},{192,224},{1,3... | collective-permute-start | bytes 688136 | tf_op jit(solution)/shard_map/while/body/eval_jaxpr/ppermute | solution.py:14
  181.7 7.8 collective-permute-start.1
  202.6 14.8 %collective-permute-start = (bf16[16,7168]{1,0:T(8,128)(2,1)S(1)}, bf16[16,7168]{1,0:T(8,128)(2,1)S(1)}, u32[]{:S(2)}, u32[]{:S(2)}) collective-permute-start(bf16[16,7168]{1,0:T(8,128)(2,1)S(1)} %fusion.233), channel_id=1, source_target_pairs={{0,32},{32,64},{64,96},{96,128},{128,160},{160,192},{192,224},{1,3... | collective-permute-start | bytes 688136 | tf_op jit(solution)/shard_map/while/body/eval_jaxpr/ppermute | solution.py:14
  210.9 6.5 collective-permute-start.1
  230.5 15.5 %collective-permute-start = (bf16[16,7168]{1,0:T(8,128)(2,1)S(1)}, bf16[16,7168]{1,0:T(8,128)(2,1)S(1)}, u32[]{:S(2)}, u32[]{:S(2)}) collective-permute-start(bf16[16,7168]{1,0:T(8,128)(2,1)S(1)} %fusion.233), channel_id=1, source_target_pairs={{0,32},{32,64},{64,96},{96,128},{128,160},{160,192},{192,224},{1,3... | collective-permute-start | bytes 688136 | tf_op jit(solution)/shard_map/while/body/eval_jaxpr/ppermute | solution.py:14
  238.6 7.4 collective-permute-start.1
  259.0 15.0 %collective-permute-start = (bf16[16,7168]{1,0:T(8,128)(2,1)S(1)}, bf16[16,7168]{1,0:T(8,128)(2,1)S(1)}, u32[]{:S(2)}, u32[]{:S(2)}) collective-permute-start(bf16[16,7168]{1,0:T(8,128)(2,1)S(1)} %fusion.233), channel_id=1, source_target_pairs={{0,32},{32,64},{64,96},{96,128},{128,160},{160,192},{192,224},{1,3... | collective-permute-start | bytes 688136 | tf_op jit(solution)/shard_map/while/body/eval_jaxpr/ppermute | solution.py:14
  267.1 6.9 collective-permute-start.1
  287.1 16.5 %collective-permute-start = (bf16[16,7168]{1,0:T(8,128)(2,1)S(1)}, bf16[16,7168]{1,0:T(8,128)(2,1)S(1)}, u32[]{:S(2)}, u32[]{:S(2)}) collective-permute-start(bf16[16,7168]{1,0:T(8,128)(2,1)S(1)} %fusion.233), channel_id=1, source_target_pairs={{0,32},{32,64},{64,96},{96,128},{128,160},{160,192},{192,224},{1,3... | collective-permute-start | bytes 688136 | tf_op jit(solution)/shard_map/while/body/eval_jaxpr/ppermute | solution.py:14
  295.3 8.3 collective-permute-start.1
  316.7 16.7 %collective-permute-start = (bf16[16,7168]{1,0:T(8,128)(2,1)S(1)}, bf16[16,7168]{1,0:T(8,128)(2,1)S(1)}, u32[]{:S(2)}, u32[]{:S(2)}) collective-permute-start(bf16[16,7168]{1,0:T(8,128)(2,1)S(1)} %fusion.233), channel_id=1, source_target_pairs={{0,32},{32,64},{64,96},{96,128},{128,160},{160,192},{192,224},{1,3... | collective-permute-start | bytes 688136 | tf_op jit(solution)/shard_map/while/body/eval_jaxpr/ppermute | solution.py:14
  324.8 8.6 collective-permute-start.1
  346.4 16.9 %collective-permute-start = (bf16[16,7168]{1,0:T(8,128)(2,1)S(1)}, bf16[16,7168]{1,0:T(8,128)(2,1)S(1)}, u32[]{:S(2)}, u32[]{:S(2)}) collective-permute-start(bf16[16,7168]{1,0:T(8,128)(2,1)S(1)} %fusion.233), channel_id=1, source_target_pairs={{0,32},{32,64},{64,96},{96,128},{128,160},{160,192},{192,224},{1,3... | collective-permute-start | bytes 688136 | tf_op jit(solution)/shard_map/while/body/eval_jaxpr/ppermute | solution.py:14
  354.5 8.8 collective-permute-start.1
  376.3 12.9 collective-permute-start
  384.6 4.7 collective-permute-start.1
  402.3 15.8 %collective-permute-start = (bf16[16,7168]{1,0:T(8,128)(2,1)S(1)}, bf16[16,7168]{1,0:T(8,128)(2,1)S(1)}, u32[]{:S(2)}, u32[]{:S(2)}) collective-permute-start(bf16[16,7168]{1,0:T(8,128)(2,1)S(1)} %fusion.233), channel_id=1, source_target_pairs={{0,32},{32,64},{64,96},{96,128},{128,160},{160,192},{192,224},{1,3... | collective-permute-start | bytes 688136 | tf_op jit(solution)/shard_map/while/body/eval_jaxpr/ppermute | solution.py:14
  410.5 7.5 collective-permute-start.1
  431.1 16.9 %collective-permute-start = (bf16[16,7168]{1,0:T(8,128)(2,1)S(1)}, bf16[16,7168]{1,0:T(8,128)(2,1)S(1)}, u32[]{:S(2)}, u32[]{:S(2)}) collective-permute-start(bf16[16,7168]{1,0:T(8,128)(2,1)S(1)} %fusion.233), channel_id=1, source_target_pairs={{0,32},{32,64},{64,96},{96,128},{128,160},{160,192},{192,224},{1,3... | collective-permute-start | bytes 688136 | tf_op jit(solution)/shard_map/while/body/eval_jaxpr/ppermute | solution.py:14
  439.3 8.7 collective-permute-start.1
  468.4 16.2 %collective-permute-start.3 = (bf16[16,56]{1,0:T(8,128)(2,1)}, bf16[16,56]{1,0:T(8,128)(2,1)}, u32[]{:S(2)}, u32[]{:S(2)}) collective-permute-start(bf16[16,56]{1,0:T(8,128)(2,1)} %multiply_convert_fusion.31), channel_id=1, source_target_pairs={{32,0},{64,32},{96,64},{128,96},{160,128},{192,160},{224,192},{33,... | collective-permute-start | bytes 5384 | tf_op jit(solution)/shard_map/while/body/eval_jaxpr/ppermute | solution.py:14
  469.7 15.0 %collective-permute-start.2 = (bf16[16,7168]{1,0:T(8,128)(2,1)}, bf16[16,7168]{1,0:T(8,128)(2,1)}, u32[]{:S(2)}, u32[]{:S(2)}) collective-permute-start(bf16[16,7168]{1,0:T(8,128)(2,1)} %fusion.261), channel_id=1, source_target_pairs={{32,0},{64,32},{96,64},{128,96},{160,128},{192,160},{224,192},{33,... | collective-permute-start | bytes 688136 | tf_op jit(solution)/shard_map/while/body/eval_jaxpr/ppermute | solution.py:14
  503.8 19.4 %collective-permute-start.3 = (bf16[16,56]{1,0:T(8,128)(2,1)}, bf16[16,56]{1,0:T(8,128)(2,1)}, u32[]{:S(2)}, u32[]{:S(2)}) collective-permute-start(bf16[16,56]{1,0:T(8,128)(2,1)} %multiply_convert_fusion.31), channel_id=1, source_target_pairs={{32,0},{64,32},{96,64},{128,96},{160,128},{192,160},{224,192},{33,... | collective-permute-start | bytes 5384 | tf_op jit(solution)/shard_map/while/body/eval_jaxpr/ppermute | solution.py:14
  505.1 18.1 %collective-permute-start.2 = (bf16[16,7168]{1,0:T(8,128)(2,1)}, bf16[16,7168]{1,0:T(8,128)(2,1)}, u32[]{:S(2)}, u32[]{:S(2)}) collective-permute-start(bf16[16,7168]{1,0:T(8,128)(2,1)} %fusion.261), channel_id=1, source_target_pairs={{32,0},{64,32},{96,64},{128,96},{160,128},{192,160},{224,192},{33,... | collective-permute-start | bytes 688136 | tf_op jit(solution)/shard_map/while/body/eval_jaxpr/ppermute | solution.py:14
  542.4 19.4 %collective-permute-start.3 = (bf16[16,56]{1,0:T(8,128)(2,1)}, bf16[16,56]{1,0:T(8,128)(2,1)}, u32[]{:S(2)}, u32[]{:S(2)}) collective-permute-start(bf16[16,56]{1,0:T(8,128)(2,1)} %multiply_convert_fusion.31), channel_id=1, source_target_pairs={{32,0},{64,32},{96,64},{128,96},{160,128},{192,160},{224,192},{33,... | collective-permute-start | bytes 5384 | tf_op jit(solution)/shard_map/while/body/eval_jaxpr/ppermute | solution.py:14
  543.7 18.1 %collective-permute-start.2 = (bf16[16,7168]{1,0:T(8,128)(2,1)}, bf16[16,7168]{1,0:T(8,128)(2,1)}, u32[]{:S(2)}, u32[]{:S(2)}) collective-permute-start(bf16[16,7168]{1,0:T(8,128)(2,1)} %fusion.261), channel_id=1, source_target_pairs={{32,0},{64,32},{96,64},{128,96},{160,128},{192,160},{224,192},{33,... | collective-permute-start | bytes 688136 | tf_op jit(solution)/shard_map/while/body/eval_jaxpr/ppermute | solution.py:14
  581.0 19.4 %collective-permute-start.3 = (bf16[16,56]{1,0:T(8,128)(2,1)}, bf16[16,56]{1,0:T(8,128)(2,1)}, u32[]{:S(2)}, u32[]{:S(2)}) collective-permute-start(bf16[16,56]{1,0:T(8,128)(2,1)} %multiply_convert_fusion.31), channel_id=1, source_target_pairs={{32,0},{64,32},{96,64},{128,96},{160,128},{192,160},{224,192},{33,... | collective-permute-start | bytes 5384 | tf_op jit(solution)/shard_map/while/body/eval_jaxpr/ppermute | solution.py:14
  582.3 18.1 %collective-permute-start.2 = (bf16[16,7168]{1,0:T(8,128)(2,1)}, bf16[16,7168]{1,0:T(8,128)(2,1)}, u32[]{:S(2)}, u32[]{:S(2)}) collective-permute-start(bf16[16,7168]{1,0:T(8,128)(2,1)} %fusion.261), channel_id=1, source_target_pairs={{32,0},{64,32},{96,64},{128,96},{160,128},{192,160},{224,192},{33,... | collective-permute-start | bytes 688136 | tf_op jit(solution)/shard_map/while/body/eval_jaxpr/ppermute | solution.py:14
  619.6 19.4 %collective-permute-start.3 = (bf16[16,56]{1,0:T(8,128)(2,1)}, bf16[16,56]{1,0:T(8,128)(2,1)}, u32[]{:S(2)}, u32[]{:S(2)}) collective-permute-start(bf16[16,56]{1,0:T(8,128)(2,1)} %multiply_convert_fusion.31), channel_id=1, source_target_pairs={{32,0},{64,32},{96,64},{128,96},{160,128},{192,160},{224,192},{33,... | collective-permute-start | bytes 5384 | tf_op jit(solution)/shard_map/while/body/eval_jaxpr/ppermute | solution.py:14
  620.9 19.1 %collective-permute-start.2 = (bf16[16,7168]{1,0:T(8,128)(2,1)}, bf16[16,7168]{1,0:T(8,128)(2,1)}, u32[]{:S(2)}, u32[]{:S(2)}) collective-permute-start(bf16[16,7168]{1,0:T(8,128)(2,1)} %fusion.261), channel_id=1, source_target_pairs={{32,0},{64,32},{96,64},{128,96},{160,128},{192,160},{224,192},{33,... | collective-permute-start | bytes 688136 | tf_op jit(solution)/shard_map/while/body/eval_jaxpr/ppermute | solution.py:14
  658.6 19.4 %collective-permute-start.3 = (bf16[16,56]{1,0:T(8,128)(2,1)}, bf16[16,56]{1,0:T(8,128)(2,1)}, u32[]{:S(2)}, u32[]{:S(2)}) collective-permute-start(bf16[16,56]{1,0:T(8,128)(2,1)} %multiply_convert_fusion.31), channel_id=1, source_target_pairs={{32,0},{64,32},{96,64},{128,96},{160,128},{192,160},{224,192},{33,... | collective-permute-start | bytes 5384 | tf_op jit(solution)/shard_map/while/body/eval_jaxpr/ppermute | solution.py:14
  659.9 19.9 %collective-permute-start.2 = (bf16[16,7168]{1,0:T(8,128)(2,1)}, bf16[16,7168]{1,0:T(8,128)(2,1)}, u32[]{:S(2)}, u32[]{:S(2)}) collective-permute-start(bf16[16,7168]{1,0:T(8,128)(2,1)} %fusion.261), channel_id=1, source_target_pairs={{32,0},{64,32},{96,64},{128,96},{160,128},{192,160},{224,192},{33,... | collective-permute-start | bytes 688136 | tf_op jit(solution)/shard_map/while/body/eval_jaxpr/ppermute | solution.py:14
  698.5 19.4 %collective-permute-start.3 = (bf16[16,56]{1,0:T(8,128)(2,1)}, bf16[16,56]{1,0:T(8,128)(2,1)}, u32[]{:S(2)}, u32[]{:S(2)}) collective-permute-start(bf16[16,56]{1,0:T(8,128)(2,1)} %multiply_convert_fusion.31), channel_id=1, source_target_pairs={{32,0},{64,32},{96,64},{128,96},{160,128},{192,160},{224,192},{33,... | collective-permute-start | bytes 5384 | tf_op jit(solution)/shard_map/while/body/eval_jaxpr/ppermute | solution.py:14
  699.8 19.9 %collective-permute-start.2 = (bf16[16,7168]{1,0:T(8,128)(2,1)}, bf16[16,7168]{1,0:T(8,128)(2,1)}, u32[]{:S(2)}, u32[]{:S(2)}) collective-permute-start(bf16[16,7168]{1,0:T(8,128)(2,1)} %fusion.261), channel_id=1, source_target_pairs={{32,0},{64,32},{96,64},{128,96},{160,128},{192,160},{224,192},{33,... | collective-permute-start | bytes 688136 | tf_op jit(solution)/shard_map/while/body/eval_jaxpr/ppermute | solution.py:14
  722.7 11.7 copy-start.13
  738.4 19.4 %collective-permute-start.3 = (bf16[16,56]{1,0:T(8,128)(2,1)}, bf16[16,56]{1,0:T(8,128)(2,1)}, u32[]{:S(2)}, u32[]{:S(2)}) collective-permute-start(bf16[16,56]{1,0:T(8,128)(2,1)} %multiply_convert_fusion.31), channel_id=1, source_target_pairs={{32,0},{64,32},{96,64},{128,96},{160,128},{192,160},{224,192},{33,... | collective-permute-start | bytes 5384 | tf_op jit(solution)/shard_map/while/body/eval_jaxpr/ppermute | solution.py:14
  739.6 19.9 %collective-permute-start.2 = (bf16[16,7168]{1,0:T(8,128)(2,1)}, bf16[16,7168]{1,0:T(8,128)(2,1)}, u32[]{:S(2)}, u32[]{:S(2)}) collective-permute-start(bf16[16,7168]{1,0:T(8,128)(2,1)} %fusion.261), channel_id=1, source_target_pairs={{32,0},{64,32},{96,64},{128,96},{160,128},{192,160},{224,192},{33,... | collective-permute-start | bytes 688136 | tf_op jit(solution)/shard_map/while/body/eval_jaxpr/ppermute | solution.py:14
  778.2 19.4 %collective-permute-start.3 = (bf16[16,56]{1,0:T(8,128)(2,1)}, bf16[16,56]{1,0:T(8,128)(2,1)}, u32[]{:S(2)}, u32[]{:S(2)}) collective-permute-start(bf16[16,56]{1,0:T(8,128)(2,1)} %multiply_convert_fusion.31), channel_id=1, source_target_pairs={{32,0},{64,32},{96,64},{128,96},{160,128},{192,160},{224,192},{33,... | collective-permute-start | bytes 5384 | tf_op jit(solution)/shard_map/while/body/eval_jaxpr/ppermute | solution.py:14
  779.5 20.0 %collective-permute-start.2 = (bf16[16,7168]{1,0:T(8,128)(2,1)}, bf16[16,7168]{1,0:T(8,128)(2,1)}, u32[]{:S(2)}, u32[]{:S(2)}) collective-permute-start(bf16[16,7168]{1,0:T(8,128)(2,1)} %fusion.261), channel_id=1, source_target_pairs={{32,0},{64,32},{96,64},{128,96},{160,128},{192,160},{224,192},{33,... | collective-permute-start | bytes 688136 | tf_op jit(solution)/shard_map/while/body/eval_jaxpr/ppermute | solution.py:14
  802.4 11.7 copy-start.13
  818.1 19.4 %collective-permute-start.3 = (bf16[16,56]{1,0:T(8,128)(2,1)}, bf16[16,56]{1,0:T(8,128)(2,1)}, u32[]{:S(2)}, u32[]{:S(2)}) collective-permute-start(bf16[16,56]{1,0:T(8,128)(2,1)} %multiply_convert_fusion.31), channel_id=1, source_target_pairs={{32,0},{64,32},{96,64},{128,96},{160,128},{192,160},{224,192},{33,... | collective-permute-start | bytes 5384 | tf_op jit(solution)/shard_map/while/body/eval_jaxpr/ppermute | solution.py:14
  819.3 19.9 %collective-permute-start.2 = (bf16[16,7168]{1,0:T(8,128)(2,1)}, bf16[16,7168]{1,0:T(8,128)(2,1)}, u32[]{:S(2)}, u32[]{:S(2)}) collective-permute-start(bf16[16,7168]{1,0:T(8,128)(2,1)} %fusion.261), channel_id=1, source_target_pairs={{32,0},{64,32},{96,64},{128,96},{160,128},{192,160},{224,192},{33,... | collective-permute-start | bytes 688136 | tf_op jit(solution)/shard_map/while/body/eval_jaxpr/ppermute | solution.py:14
  857.9 19.4 %collective-permute-start.3 = (bf16[16,56]{1,0:T(8,128)(2,1)}, bf16[16,56]{1,0:T(8,128)(2,1)}, u32[]{:S(2)}, u32[]{:S(2)}) collective-permute-start(bf16[16,56]{1,0:T(8,128)(2,1)} %multiply_convert_fusion.31), channel_id=1, source_target_pairs={{32,0},{64,32},{96,64},{128,96},{160,128},{192,160},{224,192},{33,... | collective-permute-start | bytes 5384 | tf_op jit(solution)/shard_map/while/body/eval_jaxpr/ppermute | solution.py:14
  859.2 19.9 %collective-permute-start.2 = (bf16[16,7168]{1,0:T(8,128)(2,1)}, bf16[16,7168]{1,0:T(8,128)(2,1)}, u32[]{:S(2)}, u32[]{:S(2)}) collective-permute-start(bf16[16,7168]{1,0:T(8,128)(2,1)} %fusion.261), channel_id=1, source_target_pairs={{32,0},{64,32},{96,64},{128,96},{160,128},{192,160},{224,192},{33,... | collective-permute-start | bytes 688136 | tf_op jit(solution)/shard_map/while/body/eval_jaxpr/ppermute | solution.py:14
  897.8 19.4 %collective-permute-start.3 = (bf16[16,56]{1,0:T(8,128)(2,1)}, bf16[16,56]{1,0:T(8,128)(2,1)}, u32[]{:S(2)}, u32[]{:S(2)}) collective-permute-start(bf16[16,56]{1,0:T(8,128)(2,1)} %multiply_convert_fusion.31), channel_id=1, source_target_pairs={{32,0},{64,32},{96,64},{128,96},{160,128},{192,160},{224,192},{33,... | collective-permute-start | bytes 5384 | tf_op jit(solution)/shard_map/while/body/eval_jaxpr/ppermute | solution.py:14
  899.0 19.9 %collective-permute-start.2 = (bf16[16,7168]{1,0:T(8,128)(2,1)}, bf16[16,7168]{1,0:T(8,128)(2,1)}, u32[]{:S(2)}, u32[]{:S(2)}) collective-permute-start(bf16[16,7168]{1,0:T(8,128)(2,1)} %fusion.261), channel_id=1, source_target_pairs={{32,0},{64,32},{96,64},{128,96},{160,128},{192,160},{224,192},{33,... | collective-permute-start | bytes 688136 | tf_op jit(solution)/shard_map/while/body/eval_jaxpr/ppermute | solution.py:14
  922.0 11.7 copy-start.13
  937.6 19.4 %collective-permute-start.3 = (bf16[16,56]{1,0:T(8,128)(2,1)}, bf16[16,56]{1,0:T(8,128)(2,1)}, u32[]{:S(2)}, u32[]{:S(2)}) collective-permute-start(bf16[16,56]{1,0:T(8,128)(2,1)} %multiply_convert_fusion.31), channel_id=1, source_target_pairs={{32,0},{64,32},{96,64},{128,96},{160,128},{192,160},{224,192},{33,... | collective-permute-start | bytes 5384 | tf_op jit(solution)/shard_map/while/body/eval_jaxpr/ppermute | solution.py:14
  938.9 19.9 %collective-permute-start.2 = (bf16[16,7168]{1,0:T(8,128)(2,1)}, bf16[16,7168]{1,0:T(8,128)(2,1)}, u32[]{:S(2)}, u32[]{:S(2)}) collective-permute-start(bf16[16,7168]{1,0:T(8,128)(2,1)} %fusion.261), channel_id=1, source_target_pairs={{32,0},{64,32},{96,64},{128,96},{160,128},{192,160},{224,192},{33,... | collective-permute-start | bytes 688136 | tf_op jit(solution)/shard_map/while/body/eval_jaxpr/ppermute | solution.py:14
  977.5 19.4 %collective-permute-start.3 = (bf16[16,56]{1,0:T(8,128)(2,1)}, bf16[16,56]{1,0:T(8,128)(2,1)}, u32[]{:S(2)}, u32[]{:S(2)}) collective-permute-start(bf16[16,56]{1,0:T(8,128)(2,1)} %multiply_convert_fusion.31), channel_id=1, source_target_pairs={{32,0},{64,32},{96,64},{128,96},{160,128},{192,160},{224,192},{33,... | collective-permute-start | bytes 5384 | tf_op jit(solution)/shard_map/while/body/eval_jaxpr/ppermute | solution.py:14
  978.7 20.0 %collective-permute-start.2 = (bf16[16,7168]{1,0:T(8,128)(2,1)}, bf16[16,7168]{1,0:T(8,128)(2,1)}, u32[]{:S(2)}, u32[]{:S(2)}) collective-permute-start(bf16[16,7168]{1,0:T(8,128)(2,1)} %fusion.261), channel_id=1, source_target_pairs={{32,0},{64,32},{96,64},{128,96},{160,128},{192,160},{224,192},{33,... | collective-permute-start | bytes 688136 | tf_op jit(solution)/shard_map/while/body/eval_jaxpr/ppermute | solution.py:14
  1017.3 19.4 %collective-permute-start.3 = (bf16[16,56]{1,0:T(8,128)(2,1)}, bf16[16,56]{1,0:T(8,128)(2,1)}, u32[]{:S(2)}, u32[]{:S(2)}) collective-permute-start(bf16[16,56]{1,0:T(8,128)(2,1)} %multiply_convert_fusion.31), channel_id=1, source_target_pairs={{32,0},{64,32},{96,64},{128,96},{160,128},{192,160},{224,192},{33,... | collective-permute-start | bytes 5384 | tf_op jit(solution)/shard_map/while/body/eval_jaxpr/ppermute | solution.py:14
  1018.6 19.0 %collective-permute-start.2 = (bf16[16,7168]{1,0:T(8,128)(2,1)}, bf16[16,7168]{1,0:T(8,128)(2,1)}, u32[]{:S(2)}, u32[]{:S(2)}) collective-permute-start(bf16[16,7168]{1,0:T(8,128)(2,1)} %fusion.261), channel_id=1, source_target_pairs={{32,0},{64,32},{96,64},{128,96},{160,128},{192,160},{224,192},{33,... | collective-permute-start | bytes 688136 | tf_op jit(solution)/shard_map/while/body/eval_jaxpr/ppermute | solution.py:14
  (241 other events, 1123.2 us)
Sparse Core Ops, SparseCore 0:
  1044.8 304.6 all-reduce.8
where the time goes:
time: 1380 us; the launch traced here: 1360 us
  other arithmetic  301 us (22%)
  matrix products  289 us (21%)
  starting transfers between devices  247 us (18%)
  waiting for transfers between devices  230 us (17%)
  blocking collectives  122 us (9%)
  local copies, waits for them, and re-layouts  99.2 us (7%)
  loops' own time  57.4 us (4%)
  between operations  14.1 us (1%)
    ppermute x60, starting transfers between devices, from_behind(): return lax.ppermute(block, axis, route)  247 us
    psum x1, waiting for transfers between devices, local(): lax.psum(local_sums[0].astype(jnp.bfloat16), 'dp').astype(jnp.float32)  181 us
    dot_general x105, matrix products, section_map(): jnp.dot(hidden, up_rows[layer_no], preferred_element_type=jnp.float32)  153 us
    dot_general x90, matrix products, section_map(): jnp.dot(normed, down_rows[layer_no], preferred_element_type=jnp.float32)  136 us
    psum x1, blocking collectives, local(): lax.psum(local_sums[2].astype(jnp.bfloat16), 'dp').astype(jnp.float32)  122 us
    add x15, other arithmetic, backward_tick(): running[0] + jnp.where(usable, grad_d.astype(jnp.float32), 0.0)  70.7 us
    add x15, other arithmetic, backward_tick(): running[1] + jnp.where(usable, grad_u.astype(jnp.float32), 0.0)  65.4 us
    ppermute x60, waiting for transfers between devices, from_behind(): return lax.ppermute(block, axis, route)  48.5 us
  transfers between devices with their start and end apart: 61, of which 27 were waited for; matrix products, arithmetic and copies ran while one was open for 18% of the time, Pallas kernels for 0%

commit v1 on v0

v1 whole, which is shorter than its diff:
```python
import functools
import math

import jax
import jax.numpy as jnp
from jax import lax
from jax.experimental import pallas as pl
from jax.experimental.pallas import tpu as pltpu
from jax.sharding import PartitionSpec as P

MESH = pl.DeviceIdType.MESH
F32 = jnp.float32
BF16 = jnp.bfloat16
EPSILON = 1e-05
SQUARE_EPS = 1e-06
D = 7168
RANK = 64
SHARD = 1792
BLOCKS = 14
TOKENS = 64
SECTIONS = 8
SUB = 224
AHEAD = 8
ROOT = math.sqrt(2.0 / math.pi)
CUBE = 0.044715


def dot_nn(a, b):
    return lax.dot_general(a, b, (((1,), (0,)), ((), ())), preferred_element_type=F32)


def dot_nt(a, b):
    return lax.dot_general(a, b, (((1,), (1,)), ((), ())), preferred_element_type=F32)


def dot_tn(a, b):
    return lax.dot_general(a, b, (((0,), (0,)), ((), ())), preferred_element_type=F32)


def scaled_value(v):
    square = jnp.mean(v * v, axis=-1, keepdims=True)
    factor = (2.0 * jnp.sqrt(square + SQUARE_EPS)).astype(BF16).astype(F32)
    symbols = jnp.clip(v * (1.0 / factor), -1.0, 1.0).astype(BF16).astype(F32)
    return symbols * factor


def kernel(
    ids, inp, cot, snd, rcv, dwt, upw, aux, out_d, out_u,
    w, ms, mr, ax, xs, xg, nx, dy, inv, cov, msg, pre_s, hid_s, stat, dpre_s, gp_s,
    g, cr, hs, xr, ks, zr, fs, orr,
    loc_sem, own_send, w1_recv, ax_recv, ms_recv, mr_recv, w2_send, w2_recv, w3_send, w3_recv,
    msg_send, msg_recv, r0_send, r0_recv, r1_send, r1_recv, r2_send, r2_recv, r3_send, r3_recv,
):
    sec = lax.axis_index("section")
    rep = lax.axis_index("dp")
    y = sec // 2
    zh = sec % 2
    zl = rep // 8
    xx = (rep // 2) % 4
    co = rep % 2
    z = zh * 4 + zl
    w_layer = xx // 2
    w_kind = xx % 2
    half = pl.ds(pl.multiple_of(co * 32, 32), 32)
    other_half = pl.ds(pl.multiple_of((1 - co) * 32, 32), 32)
    sibling = {"dp": rep + 1 - 2 * co}
    home_x = z // 2
    home_core = z % 2

    def columns(at):
        return pl.ds(pl.multiple_of(at * SHARD, 128), SHARD)

    def remote(src, dst, send, recv, where):
        return pltpu.make_async_remote_copy(
            src_ref=src, dst_ref=dst, send_sem=send, recv_sem=recv, device_id=where, device_id_type=MESH
        )

    def x_peer(d):
        return {"dp": zl * 8 + ((xx + d) % 4) * 2 + co}

    def z_peer(d):
        other = (z + d) % 8
        return {"section": y * 2 + other // 4, "dp": (other % 4) * 8 + xx * 2 + co}

    def home(t):
        return {"section": t, "dp": y * 8 + home_x * 2 + home_core}

    def is_home(t):
        return jnp.logical_and(t == sec, y * 8 + home_x * 2 + home_core == rep)

    mine = columns(y)
    local = [
        pltpu.make_async_copy(inp.at[0, :, :, mine], inv, loc_sem.at[0]),
        pltpu.make_async_copy(cot.at[0, :, :, mine], cov, loc_sem.at[1]),
        pltpu.make_async_copy(dwt.at[0, :, :, mine], w.at[sec, :, 0], loc_sem.at[2]),
        pltpu.make_async_copy(upw.at[0, :, :, mine], w.at[sec, :, 1], loc_sem.at[3]),
        pltpu.make_async_copy(aux.at[y], ax.at[sec], loc_sem.at[4]),
        pltpu.make_async_copy(snd.at[0, 0, pl.ds(zh * 4, 4), :, mine], ms.at[sec], loc_sem.at[5]),
        pltpu.make_async_copy(rcv.at[0, 0, pl.ds(zh * 4, 4), :, mine], mr.at[sec], loc_sem.at[6]),
    ]
    for copy in local:
        copy.start()

    barrier = pltpu.get_barrier_semaphore()

    def tell(where):
        pl.semaphore_signal(barrier, inc=1, device_id=where, device_id_type=MESH)

    for d in range(1, 8):
        tell({"section": (sec + d) % 8})
        tell(z_peer(d))
    for d in range(1, 4):
        tell(x_peer(d))
    tell(sibling)
    source_z = xx * 2 + co
    for q in range(8):
        source_section = zl * 2 + source_z // 4
        source_rep = (source_z % 4) * 8 + q
        here = jnp.logical_and(source_section == sec, source_rep == rep)

        @pl.when(jnp.logical_not(here))
        def _():
            tell({"section": source_section, "dp": source_rep})

    home_is_mine = y * 8 + home_x * 2 + home_core == rep
    pl.semaphore_wait(barrier, 7 + 7 + 3 + 1 + 8 - home_is_mine.astype(jnp.int32))

    def own_copies(d, kind):
        t2 = (sec + d) % 8
        there = columns(t2 // 2)
        slots = pl.ds((t2 % 2) * 4, 4)
        where = {"section": t2}
        if kind == 0:
            return remote(
                dwt.at[0, w_layer, half, there], w.at[sec, w_layer, 0, half], own_send.at[d - 1, 0], w1_recv.at[sec], where
            )
        if kind == 1:
            return remote(
                upw.at[0, w_layer, half, there], w.at[sec, w_layer, 1, half], own_send.at[d - 1, 0], w1_recv.at[sec], where
            )
        if kind == 2:
            return remote(aux.at[t2 // 2], ax.at[sec], own_send.at[d - 1, 1], ax_recv.at[sec], where)
        if kind == 3:
            return remote(snd.at[0, 0, slots, :, there], ms.at[sec], own_send.at[d - 1, 2], ms_recv.at[sec], where)
        return remote(rcv.at[0, 0, slots, :, there], mr.at[sec], own_send.at[d - 1, 3], mr_recv.at[sec], where)

    def each_target(action):
        def weights(d, unused):
            @pl.when(w_kind == 0)
            def _():
                action(own_copies(d, 0))

            @pl.when(w_kind == 1)
            def _():
                action(own_copies(d, 1))

            action(own_copies(d, 2))
            return unused

        def received(d, unused):
            action(own_copies(d, 4))
            return unused

        def sent(d, unused):
            action(own_copies(d, 3))
            return unused

        lax.fori_loop(1, 8, weights, 0)

        @pl.when(sec > 0)
        def _():
            lax.fori_loop(1, 8, received, 0)

        @pl.when(sec < SECTIONS - 1)
        def _():
            lax.fori_loop(1, 8, sent, 0)

    @pl.when(sec < AHEAD)
    def _():
        each_target(lambda copy: copy.start())

    for copy in local:
        copy.wait()

    for i in range(4):
        slot = zh * 4 + i
        place = jnp.int32(0)
        for m in range(8):
            place = jnp.where(ids[0, m] == slot, m, place)
        xs[0, i * 16 : (i + 1) * 16, :] = inv[place]
        dy[i * 16 : (i + 1) * 16, :] = cov[place]

    def w_part(t, kind_x):
        return w.at[t, kind_x // 2, kind_x % 2, half]

    def w2_copy(t, d):
        return remote(w_part(t, xx), w_part(t, xx), w2_send.at[t, d - 1], w2_recv.at[t, xx], x_peer(d))

    def pass_over_x(t):
        @pl.when(t != sec)
        def _():
            remote(w_part(t, xx), w_part(t, xx), own_send.at[0, 0], w1_recv.at[t], sibling).wait_recv()
            for d in range(1, 4):
                w2_copy(t, d).start()

    def w3_copy(t):
        return remote(w.at[t, :, :, half], w.at[t, :, :, half], w3_send.at[t], w3_recv.at[t], sibling)

    def w3_arrival(t):
        return remote(w.at[t, :, :, other_half], w.at[t, :, :, other_half], w3_send.at[t], w3_recv.at[t], sibling)

    def pass_to_core(t):
        @pl.when(t != sec)
        def _():
            for d in range(1, 4):
                source = (xx + d) % 4
                remote(w_part(t, source), w_part(t, source), w2_send.at[t, 0], w2_recv.at[t, source], sibling).wait_recv()
            w3_copy(t).start()

    def exchange_copy(par, d):
        return remote(
            msg.at[par, y], msg.at[par, y], msg_send.at[par, d - 1], msg_recv.at[par, y],
            {"section": ((y + d) % 4) * 2 + zh},
        )

    def exchange_start(par, value):
        msg[par, y] = value
        for d in (2, 1, 3):
            exchange_copy(par, d).start()

    def exchange_sent(par):
        for d in range(1, 4):
            exchange_copy(par, d).wait_send()

    def exchange_wait(par):
        for d in range(1, 4):
            source = (y + d) % 4
            remote(
                msg.at[par, source], msg.at[par, source], msg_send.at[par, d - 1], msg_recv.at[par, source], sibling
            ).wait_recv()

    def gain_blocks(t, l, first, count):
        rows = [ax[t, l * BLOCKS + b : l * BLOCKS + b + 1, :] for b in range(first, first + count)]
        return jnp.concatenate(rows, axis=-1) if count > 1 else rows[0]

    def gain_products(t, l):
        out = []
        for j in range(4):
            row = 28 + 2 * l + j // 2
            out.append(ax[t, row : row + 1, (j % 2) * 64 : (j % 2) * 64 + 64])
        return out

    def both(t, l):
        return w[t, l].reshape(2 * RANK, SHARD)

    pass_over_x(0)
    pass_over_x(1)
    pass_to_core(0)

    def forward(t, carry):
        @pl.when(t + AHEAD == sec)
        def _():
            each_target(lambda copy: copy.start())

        @pl.when(t != sec)
        def _():
            w3_arrival(t).wait_recv()
            remote(ax.at[t], ax.at[t], own_send.at[0, 1], ax_recv.at[t], sibling).wait_recv()

        for l in range(2):
            at = 2 * t + l
            gain = gain_blocks(t, l, 0, BLOCKS)
            centres, spreads = [], []
            for i in range(4):
                rows = slice(i * 16, (i + 1) * 16)
                xv = xs[at, rows, :].astype(F32)
                centre = jnp.sum(xv, axis=-1, keepdims=True) * (1.0 / SHARD)
                moved = xv - centre
                spreads.append(jnp.sum(moved * moved, axis=-1, keepdims=True))
                centres.append(centre)
                xg[rows, :] = (moved * gain).astype(BF16)
            centre = jnp.concatenate(centres, axis=0)
            spread = jnp.concatenate(spreads, axis=0)
            part = dot_nt(xg[...], both(t, l))
            lane = lax.broadcasted_iota(jnp.int32, (TOKENS, 128), 1)
            packed = part
            for first, number in ((64, centre), (67, spread)):
                rest = number
                for step in range(3):
                    piece = rest.astype(BF16).astype(F32)
                    packed = jnp.where(lane == first + step, piece, packed)
                    rest = rest - piece

            @pl.when(t > 0)
            def _(l=l):
                exchange_sent(l)

            exchange_start(l, packed.astype(BF16))

            if l == 0:
                @pl.when(t < SECTIONS - 2)
                def _():
                    pass_over_x(t + 2)
            else:
                @pl.when(t < SECTIONS - 1)
                def _():
                    pass_to_core(t + 1)

            exchange_wait(l)
            total = jnp.zeros((TOKENS, 128), F32)
            means = []
            spread = jnp.zeros((TOKENS, 1), F32)
            for j in range(4):
                got = msg[l, j].astype(F32)
                total = total + got
                means.append(got[:, 64:65] + got[:, 65:66] + got[:, 66:67])
                spread = spread + (got[:, 67:68] + got[:, 68:69] + got[:, 69:70])
            mean = 0.25 * (means[0] + means[1] + means[2] + means[3])
            products = gain_products(t, l)
            pre = total[:, :RANK]
            for j in range(4):
                apart = means[j] - mean
                spread = spread + SHARD * (apart * apart)
                pre = pre + apart * products[j]
            rstd = lax.rsqrt(spread * (1.0 / D) + EPSILON)
            pre = pre * rstd
            hidden = (0.5 * pre * (1.0 + jnp.tanh(ROOT * (pre + CUBE * pre * pre * pre)))).astype(BF16)
            pre_s[at] = pre
            hid_s[at] = hidden
            stat[at, 0] = jnp.broadcast_to(mean, (TOKENS, 128))
            stat[at, 1] = jnp.broadcast_to(rstd, (TOKENS, 128))

            if l == 0:
                for n in range(7):
                    cols = slice(n * 256, (n + 1) * 256)
                    branch = dot_nn(hidden, w[t, l, 1, :, cols])
                    xs[at + 1, :, cols] = (xs[at, :, cols].astype(F32) + branch).astype(BF16)
            else:
                @pl.when(t < SECTIONS - 1)
                def _(hidden=hidden, at=at):
                    @pl.when(t != sec)
                    def _():
                        remote(ms.at[t], ms.at[t], own_send.at[0, 2], ms_recv.at[t], sibling).wait_recv()

                    @pl.when(t + 1 != sec)
                    def _():
                        remote(mr.at[t + 1], mr.at[t + 1], own_send.at[0, 3], mr_recv.at[t + 1], sibling).wait_recv()

                    for n in range(7):
                        branch = dot_nn(hidden, w[t, 1, 1, :, n * 256 : (n + 1) * 256])
                        for b in range(2):
                            cols = slice(n * 256 + b * 128, n * 256 + b * 128 + 128)
                            out = (xs[at, :, cols].astype(F32) + branch[:, b * 128 : b * 128 + 128]).astype(BF16)
                            old = ms[t, :, :, cols].reshape(TOKENS, 128).astype(F32)
                            kept = mr[t + 1, :, :, cols].reshape(TOKENS, 128).astype(F32)
                            value = scaled_value(out.astype(F32) - old)
                            xs[at + 1, :, cols] = (kept + value).astype(BF16)
        return carry

    lax.fori_loop(0, SECTIONS, forward, 0)

    def begin(t, l):
        at = 2 * t + l
        par = 1 - l
        part = dot_nt(dy[...], both(t, l))
        exchange_sent(par)
        exchange_start(par, part.astype(BF16))
        pre = pre_s[at]
        tanh = jnp.tanh(ROOT * (pre + CUBE * pre * pre * pre))
        slope = 0.5 * (1.0 + tanh) + 0.5 * pre * (1.0 - tanh * tanh) * ROOT * (1.0 + 3.0 * CUBE * pre * pre)
        gp_s[...] = slope
        mean = stat[at, 0]
        rstd = stat[at, 1]
        for b in range(BLOCKS):
            cols = slice(b * 128, (b + 1) * 128)
            normed = (xs[at, :, cols].astype(F32) - mean) * rstd * gain_blocks(t, l, b, 1)
            nx[l, :, cols] = normed.astype(BF16)
        hidden = hid_s[at]
        for n in range(7):
            cols = slice(n * 256, (n + 1) * 256)
            g[t, l, 1, :, cols] = dot_tn(hidden, dy[:, cols]).astype(BF16)

    def down_gradient(t, l):
        late = dpre_s[l]
        for n in range(7):
            cols = slice(n * 256, (n + 1) * 256)
            g[t, l, 0, :, cols] = dot_tn(late, nx[l, :, cols]).astype(BF16)

    def finish(t, l):
        at = 2 * t + l
        par = 1 - l
        exchange_wait(par)
        total = jnp.zeros((TOKENS, 128), F32)
        for j in range(4):
            total = total + msg[par, j].astype(F32)
        late = (total[:, RANK:].astype(BF16).astype(F32) * gp_s[...]).astype(BF16)
        dpre_s[l] = late
        wide = late.astype(F32)

        def through():
            products = gain_products(t, l)
            across = products[0] + products[1] + products[2] + products[3]
            first = jnp.sum(wide * across, axis=-1, keepdims=True) * (1.0 / D)
            second = jnp.sum(wide * pre_s[at], axis=-1, keepdims=True) * (1.0 / D)
            mean = stat[at, 0]
            rstd = stat[at, 1]
            for n in range(7):
                moved = dot_nn(late, w[t, l, 0, :, n * 256 : (n + 1) * 256])
                for b in range(2):
                    cols = slice(n * 256 + b * 128, n * 256 + b * 128 + 128)
                    dn = moved[:, b * 128 : b * 128 + 128].astype(BF16).astype(F32)
                    hat = (xs[at, :, cols].astype(F32) - mean) * rstd
                    back = rstd * (dn * gain_blocks(t, l, 2 * n + b, 1) - first - hat * second)
                    back = (dy[:, cols].astype(F32) + back).astype(BF16)
                    if l == 0:
                        back = scaled_value(back.astype(F32)).astype(BF16)
                    dy[:, cols] = back

        if l == 0:
            pl.when(t > 0)(through)
        else:
            through()

    def r0_copy(t):
        return remote(g.at[t, :, :, other_half], cr.at[t], r0_send.at[t], r0_recv.at[t], sibling)

    def r1_copy(t, d):
        there = (xx + d) % 4
        return remote(
            hs.at[t, there // 2, there % 2], xr.at[t, 3 - d], r1_send.at[t, d - 1], r1_recv.at[t, 3 - d], x_peer(d)
        )

    def r1_start(t):
        r0_copy(t).wait_recv()
        for l in range(2):
            for kind in range(2):
                hs[t, l, kind] = (g[t, l, kind, half, :].astype(F32) + cr[t, l, kind].astype(F32)).astype(BF16)
        for d in range(1, 4):
            r1_copy(t, d).start()

    def r2_copy(t, d):
        there = (z + d) % 8
        return remote(
            ks.at[t, there], zr.at[t, 7 - d], r2_send.at[t, d - 1], r2_recv.at[t, 7 - d], z_peer(d)
        )

    def r2_start(t):
        for d in range(1, 4):
            remote(xr.at[t, d - 1], xr.at[t, d - 1], r1_send.at[t, 0], r1_recv.at[t, d - 1], sibling).wait_recv()
        for k in range(8):
            begin_at = k * SUB // 128 * 128
            shift = k * SUB - begin_at
            width = -(-(shift + SUB) // 128) * 128
            cols = slice(begin_at, begin_at + width)
            total = hs[t, w_layer, w_kind, :, cols].astype(F32)
            for d in range(3):
                total = total + xr[t, d, :, cols].astype(F32)
            if shift:
                total = pltpu.roll(total, width - shift, 1)
            ks[t, k] = total[:, :256].astype(BF16)
        for d in range(1, 8):
            r2_copy(t, d).start()

    def r3_copy(t):
        return remote(fs.at[t], orr.at[rep % 8], r3_send.at[t], r3_recv.at[rep % 8], home(t))

    def r3_start(t):
        total = ks[t, z].astype(F32)
        for d in range(7):
            remote(zr.at[t, d], zr.at[t, d], r2_send.at[t, 0], r2_recv.at[t, d], sibling).wait_recv()
            total = total + zr[t, d].astype(F32)
        fs[t] = total.astype(BF16)

        @pl.when(is_home(t))
        def _():
            orr[rep % 8] = fs[t]

        @pl.when(jnp.logical_not(is_home(t)))
        def _():
            r3_copy(t).start()

    def backward(k, carry):
        t = SECTIONS - 1 - k
        here = k < SECTIONS
        after = jnp.logical_and(k >= 1, k < SECTIONS + 1)
        later = k >= 2

        @pl.when(here)
        def _():
            begin(t, 1)

        @pl.when(after)
        def _():
            down_gradient(t + 1, 0)
            r0_copy(t + 1).start()

        @pl.when(later)
        def _():
            r2_start(t + 2)

        @pl.when(here)
        def _():
            finish(t, 1)
            begin(t, 0)
            down_gradient(t, 1)

        @pl.when(after)
        def _():
            r1_start(t + 1)

        @pl.when(later)
        def _():
            r3_start(t + 2)

        @pl.when(here)
        def _():
            finish(t, 0)

        return carry

    lax.fori_loop(0, SECTIONS + 2, backward, 0)

    for q in range(8):
        source_rep = (source_z % 4) * 8 + q
        here = jnp.logical_and(zl * 2 + source_z // 4 == sec, source_rep == rep)

        @pl.when(jnp.logical_not(here))
        def _(q=q):
            remote(orr.at[q], orr.at[q], r3_send.at[0], r3_recv.at[q], sibling).wait_recv()

    for l in range(2):
        for part in range(2):
            rows = slice(part * 32, (part + 1) * 32)
            out_d[l, rows, :] = orr[l * 4 + part][:, :SUB]
            out_u[l, rows, :] = orr[l * 4 + 2 + part][:, :SUB]

    each_target(lambda copy: copy.wait_send())
    exchange_sent(0)
    exchange_sent(1)

    def drain(t, carry):
        @pl.when(t != sec)
        def _():
            for d in range(1, 4):
                w2_copy(t, d).wait_send()
            w3_copy(t).wait_send()

        r0_copy(t).wait_send()
        for d in range(1, 4):
            r1_copy(t, d).wait_send()
        for d in range(1, 8):
            r2_copy(t, d).wait_send()

        @pl.when(jnp.logical_not(is_home(t)))
        def _():
            r3_copy(t).wait_send()

        return carry

    lax.fori_loop(0, SECTIONS, drain, 0)


def local(inputs, cotangent, send_memory, recv_memory, sample_ids, gains, down_weight, up_weight):
    dwt = jnp.swapaxes(down_weight, 2, 3)
    gain = gains[0].astype(F32)
    products = (gain[:, None, :] * dwt[0].astype(F32)).reshape(2, RANK, 4, SHARD).sum(-1)
    products = jnp.swapaxes(products, 1, 2).reshape(4, 128)
    rows = jnp.swapaxes(gain.reshape(2, 4, BLOCKS, 128), 0, 1).reshape(4, 2 * BLOCKS, 128)
    aux = jnp.concatenate([rows, jnp.broadcast_to(products, (4, 4, 128))], axis=1)

    anywhere = pl.BlockSpec(memory_space=pl.ANY)
    vmem = pl.BlockSpec(memory_space=pltpu.VMEM)
    sem = pltpu.SemaphoreType.DMA
    grad_down, grad_up = pl.pallas_call(
        kernel,
        out_shape=(
            jax.ShapeDtypeStruct((2, RANK, SUB), BF16),
            jax.ShapeDtypeStruct((2, RANK, SUB), BF16),
        ),
        in_specs=[pl.BlockSpec(memory_space=pltpu.SMEM)] + [anywhere] * 7,
        out_specs=(vmem, vmem),
        scratch_shapes=[
            pltpu.VMEM((8, 2, 2, RANK, SHARD), BF16),
            pltpu.VMEM((8, 4, 16, SHARD), BF16),
            pltpu.VMEM((8, 4, 16, SHARD), BF16),
            pltpu.VMEM((8, 32, 128), F32),
            pltpu.VMEM((16, TOKENS, SHARD), BF16),
            pltpu.VMEM((TOKENS, SHARD), BF16),
            pltpu.VMEM((2, TOKENS, SHARD), BF16),
            pltpu.VMEM((TOKENS, SHARD), BF16),
            pltpu.VMEM((8, 16, SHARD), BF16),
            pltpu.VMEM((8, 16, SHARD), BF16),
            pltpu.VMEM((2, 4, TOKENS, 128), BF16),
            pltpu.VMEM((16, TOKENS, RANK), F32),
            pltpu.VMEM((16, TOKENS, RANK), BF16),
            pltpu.VMEM((16, 2, TOKENS, 128), F32),
            pltpu.VMEM((2, TOKENS, RANK), BF16),
            pltpu.VMEM((TOKENS, RANK), F32),
            pltpu.VMEM((8, 2, 2, RANK, SHARD), BF16),
            pltpu.VMEM((8, 2, 2, 32, SHARD), BF16),
            pltpu.VMEM((8, 2, 2, 32, SHARD), BF16),
            pltpu.VMEM((8, 3, 32, SHARD), BF16),
            pltpu.VMEM((8, 8, 32, 256), BF16),
            pltpu.VMEM((8, 7, 32, 256), BF16),
            pltpu.VMEM((8, 32, 256), BF16),
            pltpu.VMEM((8, 32, 256), BF16),
            sem((7,)),
            sem((7, 4)),
            sem((8,)),
            sem((8,)),
            sem((8,)),
            sem((8,)),
            sem((8, 3)),
            sem((8, 4)),
            sem((8,)),
            sem((8,)),
            sem((2, 3)),
            sem((2, 4)),
            sem((8,)),
            sem((8,)),
            sem((8, 3)),
            sem((8, 3)),
            sem((8, 7)),
            sem((8, 7)),
            sem((8,)),
            sem((8,)),
        ],
        compiler_params=pltpu.CompilerParams(
            collective_id=0, has_side_effects=True, vmem_limit_bytes=56 * 1024 * 1024
        ),
        name="relay",
    )(sample_ids, inputs, cotangent, send_memory, recv_memory, dwt, up_weight, aux)

    start = lax.axis_index("dp") * SUB
    own_down = lax.dynamic_slice_in_dim(dwt[0], start, SUB, 2).astype(F32)
    own_gain = lax.dynamic_slice_in_dim(gain, start, SUB, 1)
    grad_gain = jnp.sum(own_down * grad_down.astype(F32), axis=1) / own_gain
    return (
        jnp.swapaxes(grad_down, 1, 2)[None],
        grad_up[None],
        grad_gain.astype(BF16)[None],
    )


def solution(mesh):
    in_specs = (
        P("dp", None, None, None),
        P("dp", None, None, None),
        P("section", "dp", None, None, None),
        P("section", "dp", None, None, None),
        P("dp", None),
        P("section", None, None),
        P("section", None, None, None),
        P("section", None, None, None),
    )
    out_specs = (
        P("section", None, "dp", None),
        P("section", None, None, "dp"),
        P("section", None, "dp"),
    )
    return jax.shard_map(local, mesh=mesh, in_specs=in_specs, out_specs=out_specs, check_vma=False)
```

time: 1380 us -> 289 us (0.21); the launches traced: 1360 us -> 289 us
  other arithmetic: 301 us -> 8.86 us
  matrix products: 289 us -> 0 us
  Pallas kernels: 0 us -> 270 us
  starting transfers between devices: 247 us -> 0 us
  waiting for transfers between devices: 230 us -> 0 us
  blocking collectives: 122 us -> 0 us
  local copies, waits for them, and re-layouts: 99.2 us -> 8.85 us
  loops' own time: 57.4 us -> 0 us
    dot_general x195 -> x0, matrix products: 289 us -> none  [the longest x105 153 us: section_map(): jnp.dot(hidden, up_rows[layer_no], preferred_element_type=jnp.float32)]
    pallas_call x0 -> x1, Pallas kernels: none -> 270 us  [local(): pl.pallas_call(kernel, out_shape=(jax.ShapeDtypeStruct((2, RANK, SUB), BF...]
    ppermute x60 -> x0, starting transfers between devices: 247 us -> none  [from_behind(): return lax.ppermute(block, axis, route)]
    psum x1 -> x0, waiting for transfers between devices: 181 us -> none  [local(): lax.psum(local_sums[0].astype(jnp.bfloat16), 'dp').astype(jnp.float32)]
    add x45 -> x0, other arithmetic: 138 us -> none  [the longest x15 70.7 us: backward_tick(): running[0] + jnp.where(usable, grad_d.astype(jnp.float32), 0.0)]
    psum x1 -> x0, blocking collectives: 122 us -> none  [local(): lax.psum(local_sums[2].astype(jnp.bfloat16), 'dp').astype(jnp.float32)]
    reduce_sum x150 -> x2, other arithmetic: 77.2 us -> 3.88 us  [the longest x1 2.85 us: local(): (gain[:, None, :] * dwt[0].astype(F32)).reshape(2, RANK, 4, SHARD).sum(-1)]
    another operation x2 -> x0, loops' own time: 57.4 us -> none  [the longest x1 43.1 us: local(): lax.scan(forward_tick, (empty_symbols, empty_factor, start_stash), jnp.ar...]
  transfers between devices with their start and end apart: 61 -> 0, of which waited for: 27 -> 0; matrix products, arithmetic and copies ran while one was open for 18% -> 0% of each run, Pallas kernels for 0% -> 0%
where the time goes in v1:
time: 289 us
  Pallas kernels  270 us (93%)
  other arithmetic  8.86 us (3%)
  local copies, waits for them, and re-layouts  8.85 us (3%)
    pallas_call x1, Pallas kernels, local(): pl.pallas_call(kernel, out_shape=(jax.ShapeDtypeStruct((2, RANK, SUB), BF...  270 us

profile of v1, /device:TPU:4, one launch (start us, length us, event | category | flops | bytes accessed | tf_op | source)
XLA Modules:
  0.0 288.8 jit_solution(13029008825178460800)
XLA Ops:
  0.6 3.7 %bitcast_convert_fusion = f32[1,2,64,7168]{3,2,1,0:T(8,128)} fusion(bf16[1,2,7168,64]{2,3,1,0:T(8,128)(2,1)} %param.14), kind=kLoop, calls=%fused_computation.7 | loop fusion | flops 917504 | bytes 5505024 | tf_op jit(solution)/shard_map/convert_element_type | solution.py:566
  4.3 0.0 copy-start
  4.3 5.7 %reshape.47 = f32[2,64,4,1792]{3,2,1,0:T(4,128)} reshape(f32[1,2,64,7168]{3,2,1,0:T(8,128)} %bitcast_convert_fusion) | data formatting | bytes 7340032 | tf_op jit(solution)/shard_map/convert_element_type | solution.py:566
  9.9 0.0 copy-done
  10.0 2.8 multiply_reduce_fusion
  12.8 0.1 copy.17
  12.9 0.1 reshape.43
  13.1 0.6 pad_maximum_fusion.aux
  13.7 270.4 %relay.1 = (bf16[2,64,224]{2,1,0:T(8,128)(2,1)}, bf16[2,64,224]{2,1,0:T(8,128)(2,1)}) custom-call(s32[1,8]{1,0:T(1,128)} %ids.1, bf16[1,8,16,7168]{3,2,1,0:T(8,128)(2,1)} %inp.1, bf16[1,8,16,7168]{3,2,1,0:T(8,128)(2,1)} %cot.1, bf16[1,1,8,16,7168]{4,3,2,1,0:T(8,128)(2,1)} %snd.1, bf16[1,1,8,16,7168]{4,3,2,1,0:T(8,128)(2,1)} %rcv.1, ...), custom_call_target="tpu_custom_call" | custom-call | tf_op jit(solution)/shard_map/relay/pallas_call | solution.py:574
  284.1 1.0 fusion
  285.2 0.7 fusion.2
  285.9 1.5 copy.21
  287.3 1.5 copy.22
  (6 shorter events, 0.1 us)
Async XLA Ops:
  4.3 5.7 %copy-start = (bf16[1,2,7168]{2,1,0:T(2,128)(2,1)S(1)}, bf16[1,2,7168]{2,1,0:T(2,128)(2,1)}, u32[]{:S(2)}) copy-start(bf16[1,2,7168]{2,1,0:T(2,128)(2,1)} %param.13) | copy-start | bytes 86020

commit v2 on v1

v2 whole, which is shorter than its diff:
```python
import functools
import math

import jax
import jax.numpy as jnp
from jax import lax
from jax.experimental import pallas as pl
from jax.experimental.pallas import tpu as pltpu
from jax.sharding import PartitionSpec as P

MESH = pl.DeviceIdType.MESH
F32 = jnp.float32
BF16 = jnp.bfloat16
EPSILON = 1e-05
SQUARE_EPS = 1e-06
D = 7168
RANK = 64
SHARD = 1792
BLOCKS = 14
TOKENS = 64
SECTIONS = 8
SUB = 224
ROOT = math.sqrt(2.0 / math.pi)
CUBE = 0.044715


def dot_nn(a, b):
    return lax.dot_general(a, b, (((1,), (0,)), ((), ())), preferred_element_type=F32)


def dot_nt(a, b):
    return lax.dot_general(a, b, (((1,), (1,)), ((), ())), preferred_element_type=F32)


def dot_tn(a, b):
    return lax.dot_general(a, b, (((0,), (0,)), ((), ())), preferred_element_type=F32)


def scaled_value(v):
    square = jnp.mean(v * v, axis=-1, keepdims=True)
    factor = (2.0 * jnp.sqrt(square + SQUARE_EPS)).astype(BF16).astype(F32)
    symbols = jnp.clip(v * (1.0 / factor), -1.0, 1.0).astype(BF16).astype(F32)
    return symbols * factor


def kernel(
    ids, inp, cot, snd, rcv, dwt, upw, gains, out_d, out_u,
    w, ms, mr, ax, px, pv, px_own, pv_own, all_gains, rw, xs, xg, dy, dy0, inv, cov, msg, msb,
    pre_s, hid_s, stat, far_s, dpre_s, gp_s,
    g, cr, hs, xr, ks, zr, fs, orr,
    loc_sem, own_send, ax_send, w1_recv, ax_recv, ms_recv, mr_recv, zw_send, zs_send, zr_send, w2_send, w2_recv, w3_send, w3_recv,
    msg_send, msg_recv, msb_send, msb_recv, r0_send, r0_recv, r1_send, r1_recv, r2_send, r2_recv, r3_send, r3_recv,
):
    sec = lax.axis_index("section")
    rep = lax.axis_index("dp")
    y = sec // 2
    zh = sec % 2
    zl = rep // 8
    xx = (rep // 2) % 4
    co = rep % 2
    z = zh * 4 + zl
    w_layer = xx // 2
    w_kind = xx % 2
    half = pl.ds(pl.multiple_of(co * 32, 32), 32)
    other_half = pl.ds(pl.multiple_of((1 - co) * 32, 32), 32)
    sibling = {"dp": rep + 1 - 2 * co}
    home_x = z // 2
    home_core = z % 2

    def columns(at):
        return pl.ds(pl.multiple_of(at * SHARD, 128), SHARD)

    def remote(src, dst, send, recv, where):
        return pltpu.make_async_remote_copy(
            src_ref=src, dst_ref=dst, send_sem=send, recv_sem=recv, device_id=where, device_id_type=MESH
        )

    def x_peer(d):
        return {"dp": zl * 8 + ((xx + d) % 4) * 2 + co}

    def z_peer(d):
        other = (z + d) % 8
        return {"section": y * 2 + other // 4, "dp": (other % 4) * 8 + xx * 2 + co}

    def home(t):
        return {"section": t, "dp": y * 8 + home_x * 2 + home_core}

    def is_home(t):
        return jnp.logical_and(t == sec, y * 8 + home_x * 2 + home_core == rep)

    mine = columns(y)
    local = [
        pltpu.make_async_copy(inp.at[0, :, :, mine], inv, loc_sem.at[0]),
        pltpu.make_async_copy(cot.at[0, :, :, mine], cov, loc_sem.at[1]),
        pltpu.make_async_copy(dwt.at[0, :, :, mine], w.at[sec, :, 0], loc_sem.at[2]),
        pltpu.make_async_copy(upw.at[0, :, :, mine], w.at[sec, :, 1], loc_sem.at[3]),
        pltpu.make_async_copy(gains, all_gains, loc_sem.at[4]),
        pltpu.make_async_copy(snd.at[0, 0, :, :, mine], ms.at[sec], loc_sem.at[5]),
        pltpu.make_async_copy(rcv.at[0, 0, :, :, mine], mr.at[sec], loc_sem.at[6]),
    ]
    for j in range(4):
        cols = slice(j * SHARD, (j + 1) * SHARD)
        local.append(pltpu.make_async_copy(dwt.at[0, :, :, cols], g.at[j, :, 0], loc_sem.at[7 + 2 * j]))
        local.append(pltpu.make_async_copy(upw.at[0, :, :, cols], g.at[j, :, 1], loc_sem.at[8 + 2 * j]))
    for copy in local:
        copy.start()

    barrier = pltpu.get_barrier_semaphore()

    def tell(where):
        pl.semaphore_signal(barrier, inc=1, device_id=where, device_id_type=MESH)

    for d in range(1, 8):
        tell({"section": (sec + d) % 8})
        tell(z_peer(d))
    for d in range(1, 4):
        tell(x_peer(d))
    tell(sibling)
    source_z = xx * 2 + co
    for q in range(8):
        source_section = zl * 2 + source_z // 4
        source_rep = (source_z % 4) * 8 + q
        here = jnp.logical_and(source_section == sec, source_rep == rep)

        @pl.when(jnp.logical_not(here))
        def _():
            tell({"section": source_section, "dp": source_rep})

    home_is_mine = y * 8 + home_x * 2 + home_core == rep
    pl.semaphore_wait(barrier, 7 + 7 + 3 + 1 + 8 - home_is_mine.astype(jnp.int32))

    own_slots = pl.ds(zh * 4, 4)
    far_slots = pl.ds(4 - zh * 4, 4)
    across = {"section": y * 2 + 1 - zh}

    def y_copy(d, kind):
        t2 = ((y + d) % 4) * 2 + zh
        there = columns((y + d) % 4)
        where = {"section": t2}
        if kind == 0:
            return remote(
                dwt.at[0, w_layer, half, there], w.at[sec, w_layer, 0, half], own_send.at[d - 1, 0], w1_recv.at[sec], where
            )
        if kind == 1:
            return remote(
                upw.at[0, w_layer, half, there], w.at[sec, w_layer, 1, half], own_send.at[d - 1, 0], w1_recv.at[sec], where
            )
        slots, number = (far_slots, 0) if kind in (2, 3) else (own_slots, 1)
        if kind in (2, 4):
            return remote(
                rcv.at[0, 0, slots, :, there], mr.at[sec, slots], own_send.at[d - 1, kind - 1], mr_recv.at[sec, number], where
            )
        return remote(
            snd.at[0, 0, slots, :, there], ms.at[sec, slots], own_send.at[d - 1, kind - 1], ms_recv.at[sec, number], where
        )

    def aux_copies(d):
        t2 = (sec + d) % 8
        where = {"section": t2}
        return (
            remote(all_gains.at[t2 // 2], ax.at[sec], ax_send.at[d - 1, 0], ax_recv.at[sec, 0], where),
            remote(px_own, px.at[sec], ax_send.at[d - 1, 1], ax_recv.at[sec, 1], where),
            remote(pv_own, pv.at[sec], ax_send.at[d - 1, 2], ax_recv.at[sec, 2], where),
        )

    def y_weights(action):
        def some(kind):
            for d in (1, 3, 2):
                action(y_copy(d, kind))

        pl.when(w_kind == 0)(lambda: some(0))
        pl.when(w_kind == 1)(lambda: some(1))

    def y_memories(action):
        def some(kind):
            for d in (1, 3, 2):
                action(y_copy(d, kind))

        for kind in range(2, 6):
            pl.when(sec > 0 if kind % 2 == 0 else sec < SECTIONS - 1)(functools.partial(some, kind))

    def y_aux(action):
        for d in range(1, 8):
            for copy in aux_copies(d):
                action(copy)

    y_weights(lambda copy: copy.start())
    for copy in local:
        copy.wait()

    def gain_blocks(rows_ref, l, first, count):
        rows = [rows_ref[l * BLOCKS + b : l * BLOCKS + b + 1, :] for b in range(first, first + count)]
        return jnp.concatenate(rows, axis=-1) if count > 1 else rows[0]

    def fold(weights, rows_ref, into):
        for l in range(2):
            gained = weights[l, 0].astype(F32) * gain_blocks(rows_ref, l, 0, BLOCKS)
            into[l * RANK : (l + 1) * RANK, :] = gained.astype(BF16)
        into[2 * RANK :, :] = weights[0, 1]

    ones = jnp.ones((16, SHARD), BF16)
    products = jnp.zeros((RANK, 2 * RANK), F32)
    up_sum = jnp.zeros((RANK, 16), F32)
    whole = jnp.zeros((16, 3 * RANK), F32)
    for j in range(4):
        fold(g.at[j], all_gains.at[j], rw.at[0])
        here_sums = dot_nt(ones, rw[0])
        whole = whole + here_sums
        px_own[2 * j : 2 * j + 1, :] = here_sums[:1, : 2 * RANK]
        px_own[2 * j + 1 : 2 * j + 2, :] = jnp.concatenate([here_sums[:1, 2 * RANK :], jnp.zeros((1, RANK), F32)], axis=-1)
        up = rw[0, 2 * RANK :, :]
        products = products + dot_nt(up, rw[0, RANK:, :])
        up_sum = up_sum + dot_nt(up, ones)
    products = products - up_sum[:, :1] * (whole[:1, RANK:] * (1.0 / D))
    pv_own[...] = products.astype(BF16)
    ax[sec] = all_gains[y]
    px[sec] = px_own[...]
    pv[sec] = pv_own[...]
    y_aux(lambda copy: copy.start())
    y_memories(lambda copy: copy.start())

    for i in range(4):
        slot = zh * 4 + i
        place = jnp.int32(0)
        for m in range(8):
            place = jnp.where(ids[0, m] == slot, m, place)
        xs[0, i * 16 : (i + 1) * 16, :] = inv[place]
        dy[i * 16 : (i + 1) * 16, :] = cov[place]

    def w_part(t, kind_x):
        return w.at[t, kind_x // 2, kind_x % 2, half]

    def w2_copy(t, d):
        return remote(w_part(t, xx), w_part(t, xx), w2_send.at[t, d - 1], w2_recv.at[t, xx], x_peer(d))

    def zw_copy(t):
        return remote(w_part(t, xx), w_part(t, xx), zw_send.at[t], w1_recv.at[t], across)

    def zs_copy(t):
        return remote(ms.at[t, far_slots], ms.at[t, far_slots], zs_send.at[t], ms_recv.at[t, 1], across)

    def zr_copy(t):
        return remote(mr.at[t, far_slots], mr.at[t, far_slots], zr_send.at[t], mr_recv.at[t, 1], across)

    def ms_wait(t, number):
        slots = own_slots if number else far_slots

        @pl.when(t != sec)
        def _():
            remote(ms.at[t, slots], ms.at[t, slots], zs_send.at[t], ms_recv.at[t, number], sibling).wait_recv()

    def mr_wait(t, number):
        slots = own_slots if number else far_slots

        @pl.when(t != sec)
        def _():
            remote(mr.at[t, slots], mr.at[t, slots], zr_send.at[t], mr_recv.at[t, number], sibling).wait_recv()

    def relay(b):
        @pl.when(b % 2 == zh)
        def _():
            ms_wait(b, 0)
            zs_copy(b).start()

        @pl.when(b % 2 != zh)
        def _():
            mr_wait(b + 1, 0)
            zr_copy(b + 1).start()

    def over_x(t):
        @pl.when(t != sec)
        def _():
            remote(w_part(t, xx), w_part(t, xx), own_send.at[0, 0], w1_recv.at[t], sibling).wait_recv()

        pl.when(t % 2 == zh)(lambda: zw_copy(t).start())

        @pl.when(t != sec)
        def _():
            for d in range(1, 4):
                w2_copy(t, d).start()

    def over_x_from_far(t):
        pl.when(t % 2 != zh)(lambda: over_x(t))

    def w3_copy(t):
        return remote(w.at[t, :, :, half], w.at[t, :, :, half], w3_send.at[t], w3_recv.at[t], sibling)

    def w3_arrival(t):
        return remote(w.at[t, :, :, other_half], w.at[t, :, :, other_half], w3_send.at[t], w3_recv.at[t], sibling)

    def pass_to_core(t):
        @pl.when(t != sec)
        def _():
            for d in range(1, 4):
                source = (xx + d) % 4
                remote(w_part(t, source), w_part(t, source), w2_send.at[t, 0], w2_recv.at[t, source], sibling).wait_recv()
            w3_copy(t).start()

    def exchange_copy(buffers, par, d):
        held, send, recv = buffers
        return remote(
            held.at[par, y], held.at[par, y], send.at[par, d - 1], recv.at[par, y], {"section": ((y + d) % 4) * 2 + zh}
        )

    def exchange_start(buffers, par, value):
        buffers[0][par, y] = value
        for d in (2, 1, 3):
            exchange_copy(buffers, par, d).start()

    def exchange_sent(buffers, par):
        for d in range(1, 4):
            exchange_copy(buffers, par, d).wait_send()

    def exchange_wait(buffers, par):
        held, send, recv = buffers
        for d in range(1, 4):
            source = (y + d) % 4
            remote(
                held.at[par, source], held.at[par, source], send.at[par, d - 1], recv.at[par, source], sibling
            ).wait_recv()

    ahead = (msg, msg_send, msg_recv)
    back = (msb, msb_send, msb_recv)

    def sums_of(t, j):
        return px[t, 2 * j : 2 * j + 1, :], px[t, 2 * j + 1 : 2 * j + 2, :RANK]

    def gelu(pre):
        return (0.5 * pre * (1.0 + jnp.tanh(ROOT * (pre + CUBE * pre * pre * pre)))).astype(BF16)

    def gelu_slope(pre):
        tanh = jnp.tanh(ROOT * (pre + CUBE * pre * pre * pre))
        return 0.5 * (1.0 + tanh) + 0.5 * pre * (1.0 - tanh * tanh) * ROOT * (1.0 + 3.0 * CUBE * pre * pre)

    def ready(t):
        @pl.when(t != sec)
        def _():
            w3_arrival(t).wait_recv()
            for n, held in enumerate((ax, px, pv)):
                remote(held.at[t], held.at[t], ax_send.at[0, n], ax_recv.at[t, n], sibling).wait_recv()

        fold(w.at[t], ax.at[t], rw.at[t % 2])

    def first(i, carry):
        over_x(2 * i + zh)
        pl.when(i > 0)(lambda: relay(2 * i - 1))
        relay(2 * i)
        return carry

    lax.fori_loop(0, 4, first, 0)
    over_x_from_far(0)
    over_x_from_far(1)
    over_x_from_far(2)
    pass_to_core(0)
    pass_to_core(1)
    ready(0)

    def wide(column):
        return jnp.broadcast_to(column, (TOKENS, 128))

    def forward(t, carry):
        at = 2 * t
        par = t % 2
        centres, spreads = [], []
        for i in range(4):
            rows = slice(i * 16, (i + 1) * 16)
            xv = xs[at, rows, :].astype(F32)
            centre = jnp.sum(xv, axis=-1, keepdims=True) * (1.0 / SHARD)
            moved = xv - centre
            spreads.append(jnp.sum(moved * moved, axis=-1, keepdims=True))
            centres.append(centre)
            xg[rows, :] = moved.astype(BF16)
        centre = jnp.concatenate(centres, axis=0)
        spread = jnp.concatenate(spreads, axis=0)
        part = dot_nt(xg[...], rw[par])
        lane = lax.broadcasted_iota(jnp.int32, (TOKENS, RANK), 1)
        packed = jnp.zeros((TOKENS, RANK), F32)
        for start, number in ((0, centre), (3, spread)):
            rest = number
            for step in range(3):
                piece = rest.astype(BF16).astype(F32)
                packed = jnp.where(lane == start + step, piece, packed)
                rest = rest - piece

        pl.when(t > 1)(lambda: exchange_sent(ahead, par))
        exchange_start(ahead, par, jnp.concatenate([part, packed], axis=-1).astype(BF16))

        pl.when(t < SECTIONS - 3)(lambda: over_x_from_far(t + 3))
        pl.when(t < SECTIONS - 2)(lambda: pass_to_core(t + 2))
        pl.when(t < SECTIONS - 1)(lambda: ready(t + 1))

        exchange_wait(ahead, par)
        first = jnp.zeros((TOKENS, 2 * RANK), F32)
        second = jnp.zeros((TOKENS, 2 * RANK), F32)
        means = []
        spread = jnp.zeros((TOKENS, 1), F32)
        for j in range(4):
            first = first + msg[par, j, :, : 2 * RANK].astype(F32)
            got = msg[par, j, :, 2 * RANK :].astype(F32)
            second = second + got
            means.append(got[:, 64:65] + got[:, 65:66] + got[:, 66:67])
            spread = spread + (got[:, 67:68] + got[:, 68:69] + got[:, 69:70])
        mean = 0.25 * (means[0] + means[1] + means[2] + means[3])
        second = second[:, :RANK]
        up_mean = jnp.zeros((1, RANK), F32)
        for j in range(4):
            apart = means[j] - mean
            spread = spread + SHARD * (apart * apart)
            sums, up_sums = sums_of(t, j)
            first = first + apart * sums
            second = second + apart * up_sums
            up_mean = up_mean + up_sums * (1.0 / D)
        rstd = lax.rsqrt(spread * (1.0 / D) + EPSILON)
        pre = first[:, :RANK] * rstd
        hidden = gelu(pre)
        moved = dot_nn(hidden, pv[t])
        hidden_wide = hidden.astype(F32)
        far = second + moved[:, RANK:]
        spread1 = jnp.maximum(spread + jnp.sum(hidden_wide * (second + far), axis=-1, keepdims=True), 0.0)
        rstd1 = lax.rsqrt(spread1 * (1.0 / D) + EPSILON)
        mean1 = mean + jnp.sum(hidden_wide * up_mean, axis=-1, keepdims=True)
        pre1 = (first[:, RANK:] + moved[:, :RANK]) * rstd1
        hidden1 = gelu(pre1)
        pre_s[at] = pre
        pre_s[at + 1] = pre1
        hid_s[at] = hidden
        hid_s[at + 1] = hidden1
        far_s[t] = far
        stat[at, 0] = wide(mean)
        stat[at, 1] = wide(rstd)
        stat[at + 1, 0] = wide(mean1)
        stat[at + 1, 1] = wide(rstd1)

        def next_layer(n):
            cols = slice(n * 256, (n + 1) * 256)
            branch = dot_nn(hidden, w[t, 0, 1, :, cols])
            middle = (xs[at, :, cols].astype(F32) + branch).astype(BF16)
            xs[at + 1, :, cols] = middle
            return middle

        @pl.when(t == SECTIONS - 1)
        def _():
            for n in range(7):
                next_layer(n)

        @pl.when(t < SECTIONS - 1)
        def _():
            ms_wait(t, 1)
            mr_wait(t + 1, 1)
            for n in range(7):
                middle = next_layer(n).astype(F32)
                branch = dot_nn(hidden1, w[t, 1, 1, :, n * 256 : (n + 1) * 256])
                out = (middle + branch).astype(BF16).astype(F32)
                for b in range(2):
                    cols = slice(n * 256 + b * 128, n * 256 + b * 128 + 128)
                    old = ms[t, own_slots, :, cols].reshape(TOKENS, 128).astype(F32)
                    kept = mr[t + 1, own_slots, :, cols].reshape(TOKENS, 128).astype(F32)
                    value = scaled_value(out[:, b * 128 : b * 128 + 128] - old)
                    xs[at + 2, :, cols] = (kept + value).astype(BF16)

        return carry

    lax.fori_loop(0, SECTIONS, forward, 0)
    exchange_sent(ahead, 0)
    exchange_sent(ahead, 1)

    def begin(t, par):
        part = dot_nt(dy[...], w[t, :, 1].reshape(2 * RANK, SHARD))
        pl.when(t < SECTIONS - 2)(lambda: exchange_sent(back, par))
        exchange_start(back, par, part.astype(BF16))
        gp_s[0] = gelu_slope(pre_s[2 * t])
        gp_s[1] = gelu_slope(pre_s[2 * t + 1])
        hidden = hid_s[2 * t + 1]
        for n in range(7):
            cols = slice(n * 256, (n + 1) * 256)
            g[t, 1, 1, :, cols] = dot_tn(hidden, dy[:, cols]).astype(BF16)

    def gradients(t):
        hidden = hid_s[2 * t]
        for n in range(7):
            cols = slice(n * 256, (n + 1) * 256)
            for l in range(2):
                at = 2 * t + l
                pieces = []
                for b in (2 * n, 2 * n + 1):
                    part = xs[at, :, b * 128 : (b + 1) * 128].astype(F32)
                    pieces.append((part - stat[at, 0]) * stat[at, 1] * gain_blocks(ax.at[t], l, b, 1))
                normed = jnp.concatenate(pieces, axis=-1).astype(BF16)
                g[t, l, 0, :, cols] = dot_tn(dpre_s[l], normed).astype(BF16)
            g[t, 0, 1, :, cols] = dot_tn(hidden, dy0[:, cols]).astype(BF16)

    def finish(t, par):
        exchange_wait(back, par)
        total = jnp.zeros((TOKENS, 2 * RANK), F32)
        for j in range(4):
            total = total + msb[par, j].astype(F32)
        both_sums = px[t, 0:1, :] + px[t, 2:3, :] + px[t, 4:5, :] + px[t, 6:7, :]

        def row_means(late, l):
            numbers = late.astype(F32)
            one = jnp.sum(numbers * both_sums[:, l * RANK : (l + 1) * RANK], axis=-1, keepdims=True) * (1.0 / D)
            two = jnp.sum(numbers * pre_s[2 * t + l], axis=-1, keepdims=True) * (1.0 / D)
            return one, two

        late1 = (total[:, RANK:].astype(BF16).astype(F32) * gp_s[1]).astype(BF16)
        dpre_s[1] = late1
        one1, two1 = row_means(late1, 1)
        mean1, rstd1 = stat[2 * t + 1, 0], stat[2 * t + 1, 1]
        column = rstd1[:, :RANK]
        inner = total[:, :RANK] + column * (dot_nt(late1, pv[t, :, :RANK]) - two1 * column * far_s[t])
        late0 = (inner.astype(BF16).astype(F32) * gp_s[0]).astype(BF16)
        dpre_s[0] = late0
        for n in range(7):
            moved = dot_nn(late1, w[t, 1, 0, :, n * 256 : (n + 1) * 256])
            for b in range(2):
                cols = slice(n * 256 + b * 128, n * 256 + b * 128 + 128)
                dn = moved[:, b * 128 : b * 128 + 128].astype(BF16).astype(F32)
                hat = (xs[2 * t + 1, :, cols].astype(F32) - mean1) * rstd1
                step = rstd1 * (dn * gain_blocks(ax.at[t], 1, 2 * n + b, 1) - one1 - hat * two1)
                dy0[:, cols] = (dy[:, cols].astype(F32) + step).astype(BF16)

        @pl.when(t > 0)
        def _():
            one0, two0 = row_means(late0, 0)
            mean0, rstd0 = stat[2 * t, 0], stat[2 * t, 1]
            for n in range(7):
                moved = dot_nn(late0, w[t, 0, 0, :, n * 256 : (n + 1) * 256])
                for b in range(2):
                    cols = slice(n * 256 + b * 128, n * 256 + b * 128 + 128)
                    dn = moved[:, b * 128 : b * 128 + 128].astype(BF16).astype(F32)
                    hat = (xs[2 * t, :, cols].astype(F32) - mean0) * rstd0
                    step = rstd0 * (dn * gain_blocks(ax.at[t], 0, 2 * n + b, 1) - one0 - hat * two0)
                    out = (dy0[:, cols].astype(F32) + step).astype(BF16).astype(F32)
                    dy[:, cols] = scaled_value(out).astype(BF16)

    def r0_copy(t):
        return remote(g.at[t, :, :, other_half], cr.at[t], r0_send.at[t], r0_recv.at[t], sibling)

    def r1_copy(t, d):
        there = (xx + d) % 4
        return remote(
            hs.at[t, there // 2, there % 2], xr.at[t, 3 - d], r1_send.at[t, d - 1], r1_recv.at[t, 3 - d], x_peer(d)
        )

    def r1_start(t):
        r0_copy(t).wait_recv()
        for l in range(2):
            for kind in range(2):
                hs[t, l, kind] = (g[t, l, kind, half, :].astype(F32) + cr[t, l, kind].astype(F32)).astype(BF16)
        for d in range(1, 4):
            r1_copy(t, d).start()

    def r2_copy(t, d):
        there = (z + d) % 8
        return remote(
            ks.at[t, there], zr.at[t, 7 - d], r2_send.at[t, d - 1], r2_recv.at[t, 7 - d], z_peer(d)
        )

    def r2_start(t):
        for d in range(1, 4):
            remote(xr.at[t, d - 1], xr.at[t, d - 1], r1_send.at[t, 0], r1_recv.at[t, d - 1], sibling).wait_recv()
        for k in range(8):
            begin_at = k * SUB // 128 * 128
            shift = k * SUB - begin_at
            width = -(-(shift + SUB) // 128) * 128
            cols = slice(begin_at, begin_at + width)
            total = hs[t, w_layer, w_kind, :, cols].astype(F32)
            for d in range(3):
                total = total + xr[t, d, :, cols].astype(F32)
            if shift:
                total = pltpu.roll(total, width - shift, 1)
            ks[t, k] = total[:, :256].astype(BF16)
        for d in range(1, 8):
            r2_copy(t, d).start()

    def r3_copy(t):
        return remote(fs.at[t], orr.at[rep % 8], r3_send.at[t], r3_recv.at[rep % 8], home(t))

    def r3_start(t):
        total = ks[t, z].astype(F32)
        for d in range(7):
            remote(zr.at[t, d], zr.at[t, d], r2_send.at[t, 0], r2_recv.at[t, d], sibling).wait_recv()
            total = total + zr[t, d].astype(F32)
        fs[t] = total.astype(BF16)

        @pl.when(is_home(t))
        def _():
            orr[rep % 8] = fs[t]

        @pl.when(jnp.logical_not(is_home(t)))
        def _():
            r3_copy(t).start()

    def backward(k, carry):
        t = SECTIONS - 1 - k
        par = k % 2

        def within(first):
            return jnp.logical_and(k >= first, k < SECTIONS + first)

        pl.when(k < SECTIONS)(lambda: begin(t, par))

        @pl.when(within(1))
        def _():
            gradients(t + 1)
            r0_copy(t + 1).start()

        pl.when(within(2))(lambda: r1_start(t + 2))
        pl.when(within(3))(lambda: r2_start(t + 3))
        pl.when(within(4))(lambda: r3_start(t + 4))
        pl.when(k < SECTIONS)(lambda: finish(t, par))
        return carry

    lax.fori_loop(0, SECTIONS + 4, backward, 0)

    for q in range(8):
        source_rep = (source_z % 4) * 8 + q
        here = jnp.logical_and(zl * 2 + source_z // 4 == sec, source_rep == rep)

        @pl.when(jnp.logical_not(here))
        def _(q=q):
            remote(orr.at[q], orr.at[q], r3_send.at[0], r3_recv.at[q], sibling).wait_recv()

    for l in range(2):
        for part in range(2):
            rows = slice(part * 32, (part + 1) * 32)
            out_d[l, rows, :] = orr[l * 4 + part][:, :SUB]
            out_u[l, rows, :] = orr[l * 4 + 2 + part][:, :SUB]

    y_weights(lambda copy: copy.wait_send())
    y_aux(lambda copy: copy.wait_send())
    y_memories(lambda copy: copy.wait_send())
    exchange_sent(back, 0)
    exchange_sent(back, 1)

    def drain(t, carry):
        @pl.when(t % 2 == zh)
        def _():
            zw_copy(t).wait_send()

            @pl.when(t < SECTIONS - 1)
            def _():
                zs_copy(t).wait_send()

            @pl.when(t > 0)
            def _():
                zr_copy(t).wait_send()

        @pl.when(t != sec)
        def _():
            for d in range(1, 4):
                w2_copy(t, d).wait_send()
            w3_copy(t).wait_send()

        r0_copy(t).wait_send()
        for d in range(1, 4):
            r1_copy(t, d).wait_send()
        for d in range(1, 8):
            r2_copy(t, d).wait_send()

        @pl.when(jnp.logical_not(is_home(t)))
        def _():
            r3_copy(t).wait_send()

        return carry

    lax.fori_loop(0, SECTIONS, drain, 0)


def local(inputs, cotangent, send_memory, recv_memory, sample_ids, gains, down_weight, up_weight):
    dwt = jnp.swapaxes(down_weight, 2, 3)
    gain = gains[0].astype(F32)
    rows = jnp.swapaxes(gain.reshape(2, 4, BLOCKS, 128), 0, 1).reshape(4, 2 * BLOCKS, 128)
    rows = jnp.pad(rows, ((0, 0), (0, 4), (0, 0)))

    anywhere = pl.BlockSpec(memory_space=pl.ANY)
    vmem = pl.BlockSpec(memory_space=pltpu.VMEM)
    sem = pltpu.SemaphoreType.DMA
    grad_down, grad_up = pl.pallas_call(
        kernel,
        out_shape=(
            jax.ShapeDtypeStruct((2, RANK, SUB), BF16),
            jax.ShapeDtypeStruct((2, RANK, SUB), BF16),
        ),
        in_specs=[pl.BlockSpec(memory_space=pltpu.SMEM)] + [anywhere] * 7,
        out_specs=(vmem, vmem),
        scratch_shapes=[
            pltpu.VMEM((8, 2, 2, RANK, SHARD), BF16),
            pltpu.VMEM((8, 8, 16, SHARD), BF16),
            pltpu.VMEM((8, 8, 16, SHARD), BF16),
            pltpu.VMEM((8, 32, 128), F32),
            pltpu.VMEM((8, 8, 128), F32),
            pltpu.VMEM((8, RANK, 128), BF16),
            pltpu.VMEM((8, 128), F32),
            pltpu.VMEM((RANK, 128), BF16),
            pltpu.VMEM((4, 32, 128), F32),
            pltpu.VMEM((2, 3 * RANK, SHARD), BF16),
            pltpu.VMEM((16, TOKENS, SHARD), BF16),
            pltpu.VMEM((TOKENS, SHARD), BF16),
            pltpu.VMEM((TOKENS, SHARD), BF16),
            pltpu.VMEM((TOKENS, SHARD), BF16),
            pltpu.VMEM((8, 16, SHARD), BF16),
            pltpu.VMEM((8, 16, SHARD), BF16),
            pltpu.VMEM((2, 4, TOKENS, 256), BF16),
            pltpu.VMEM((2, 4, TOKENS, 128), BF16),
            pltpu.VMEM((16, TOKENS, RANK), F32),
            pltpu.VMEM((16, TOKENS, RANK), BF16),
            pltpu.VMEM((16, 2, TOKENS, 128), F32),
            pltpu.VMEM((8, TOKENS, RANK), F32),
            pltpu.VMEM((2, TOKENS, RANK), BF16),
            pltpu.VMEM((2, TOKENS, RANK), F32),
            pltpu.VMEM((8, 2, 2, RANK, SHARD), BF16),
            pltpu.VMEM((8, 2, 2, 32, SHARD), BF16),
            pltpu.VMEM((8, 2, 2, 32, SHARD), BF16),
            pltpu.VMEM((8, 3, 32, SHARD), BF16),
            pltpu.VMEM((8, 8, 32, 256), BF16),
            pltpu.VMEM((8, 7, 32, 256), BF16),
            pltpu.VMEM((8, 32, 256), BF16),
            pltpu.VMEM((8, 32, 256), BF16),
            sem((15,)),
            sem((3, 5)),
            sem((7, 3)),
            sem((8,)),
            sem((8, 3)),
            sem((8, 2)),
            sem((8, 2)),
            sem((8,)),
            sem((8,)),
            sem((8,)),
            sem((8, 3)),
            sem((8, 4)),
            sem((8,)),
            sem((8,)),
            sem((2, 3)),
            sem((2, 4)),
            sem((2, 3)),
            sem((2, 4)),
            sem((8,)),
            sem((8,)),
            sem((8, 3)),
            sem((8, 3)),
            sem((8, 7)),
            sem((8, 7)),
            sem((8,)),
            sem((8,)),
        ],
        compiler_params=pltpu.CompilerParams(
            collective_id=0, has_side_effects=True, vmem_limit_bytes=56 * 1024 * 1024
        ),
        name="relay",
    )(sample_ids, inputs, cotangent, send_memory, recv_memory, dwt, up_weight, rows)

    start = lax.axis_index("dp") * SUB
    own_down = lax.dynamic_slice_in_dim(dwt[0], start, SUB, 2).astype(F32)
    own_gain = lax.dynamic_slice_in_dim(gain, start, SUB, 1)
    grad_gain = jnp.sum(own_down * grad_down.astype(F32), axis=1) / own_gain
    return (
        jnp.swapaxes(grad_down, 1, 2)[None],
        grad_up[None],
        grad_gain.astype(BF16)[None],
    )


def solution(mesh):
    in_specs = (
        P("dp", None, None, None),
        P("dp", None, None, None),
        P("section", "dp", None, None, None),
        P("section", "dp", None, None, None),
        P("dp", None),
        P("section", None, None),
        P("section", None, None, None),
        P("section", None, None, None),
    )
    out_specs = (
        P("section", None, "dp", None),
        P("section", None, None, "dp"),
        P("section", None, "dp"),
    )
    return jax.shard_map(local, mesh=mesh, in_specs=in_specs, out_specs=out_specs, check_vma=False)
```

time: 289 us -> 214 us (0.74)
  Pallas kernels: 270 us -> 206 us
  other arithmetic: 8.86 us -> 3.01 us
  local copies, waits for them, and re-layouts: 8.85 us -> 3.75 us
    pallas_call x1, Pallas kernels: 270 us -> 206 us  [local(): pl.pallas_call(kernel, out_shape=(jax.ShapeDtypeStruct((2, RANK, SUB), BF...]
    convert_element_type x1 -> x0, local copies, waits for them, and re-layouts: 5.65 us -> none  [local(): dwt[0].astype(F32)]
    convert_element_type x1 -> x0, other arithmetic: 3.66 us -> none  [local(): dwt[0].astype(F32)]
where the time goes in v2:
time: 214 us; the launch traced here: 213 us
  Pallas kernels  206 us (96%)
  local copies, waits for them, and re-layouts  3.75 us (2%)
  other arithmetic  3.01 us (1%)
    pallas_call x1, Pallas kernels, local(): pl.pallas_call(kernel, out_shape=(jax.ShapeDtypeStruct((2, RANK, SUB), BF...  206 us

profile of v2, /device:TPU:4, one launch (start us, length us, event | category | flops | bytes accessed | tf_op | source)
XLA Modules:
  0.0 213.5 jit_solution(6207115785396993524)
XLA Ops:
  0.6 0.8 convert_element_type.25
  1.5 0.6 pad_convert_fusion.gains
  2.1 206.1 %relay.1 = (bf16[2,64,224]{2,1,0:T(8,128)(2,1)}, bf16[2,64,224]{2,1,0:T(8,128)(2,1)}) custom-call(s32[1,8]{1,0:T(1,128)} %ids.1, bf16[1,8,16,7168]{3,2,1,0:T(8,128)(2,1)} %inp.1, bf16[1,8,16,7168]{3,2,1,0:T(8,128)(2,1)} %cot.1, bf16[1,1,8,16,7168]{4,3,2,1,0:T(8,128)(2,1)} %snd.1, bf16[1,1,8,16,7168]{4,3,2,1,0:T(8,128)(2,1)} %rcv.1, ...), custom_call_target="tpu_custom_call" | custom-call | tf_op jit(solution)/shard_map/relay/pallas_call | solution.py:679
  208.2 1.0 fusion
  209.2 1.3 fusion.2
  210.5 1.5 copy.16
  212.0 1.5 copy.17
  (2 shorter events, 0.0 us)

commit v3 on v2

--- a/solution.py
+++ b/solution.py
@@ -44,11 +44,11 @@
 
 
 def kernel(
-    ids, inp, cot, snd, rcv, dwt, upw, gains, out_d, out_u,
-    w, ms, mr, ax, px, pv, px_own, pv_own, all_gains, rw, xs, xg, dy, dy0, inv, cov, msg, msb,
+    ids, inp, cot, snd, rcv, dwt, upw, gains, out_d, out_u, out_g,
+    w, ms, mr, ax, px, pv, px_own, pv_own, all_gains, all_wide, ax_wide, own_down, rw, xs, xg, dy, dy0, inv, cov, msg, msb,
     pre_s, hid_s, stat, far_s, dpre_s, gp_s,
     g, cr, hs, xr, ks, zr, fs, orr,
-    loc_sem, own_send, ax_send, w1_recv, ax_recv, ms_recv, mr_recv, zw_send, zs_send, zr_send, w2_send, w2_recv, w3_send, w3_recv,
+    loc_sem, own_send, ax_send, w1_recv, wz_recv, ax_recv, ms_recv, mr_recv, zw_send, zs_send, zr_send, w2_send, w2_recv, w3_send, w3_recv,
     msg_send, msg_recv, msb_send, msb_recv, r0_send, r0_recv, r1_send, r1_recv, r2_send, r2_recv, r3_send, r3_recv,
 ):
     sec = lax.axis_index("section")
@@ -94,14 +94,13 @@
         pltpu.make_async_copy(cot.at[0, :, :, mine], cov, loc_sem.at[1]),
         pltpu.make_async_copy(dwt.at[0, :, :, mine], w.at[sec, :, 0], loc_sem.at[2]),
         pltpu.make_async_copy(upw.at[0, :, :, mine], w.at[sec, :, 1], loc_sem.at[3]),
-        pltpu.make_async_copy(gains, all_gains, loc_sem.at[4]),
-        pltpu.make_async_copy(snd.at[0, 0, :, :, mine], ms.at[sec], loc_sem.at[5]),
-        pltpu.make_async_copy(rcv.at[0, 0, :, :, mine], mr.at[sec], loc_sem.at[6]),
+        pltpu.make_async_copy(snd.at[0, 0, :, :, mine], ms.at[sec], loc_sem.at[4]),
+        pltpu.make_async_copy(rcv.at[0, 0, :, :, mine], mr.at[sec], loc_sem.at[5]),
     ]
     for j in range(4):
         cols = slice(j * SHARD, (j + 1) * SHARD)
-        local.append(pltpu.make_async_copy(dwt.at[0, :, :, cols], g.at[j, :, 0], loc_sem.at[7 + 2 * j]))
-        local.append(pltpu.make_async_copy(upw.at[0, :, :, cols], g.at[j, :, 1], loc_sem.at[8 + 2 * j]))
+        local.append(pltpu.make_async_copy(dwt.at[0, :, :, cols], g.at[j, :, 0], loc_sem.at[6 + 2 * j]))
+        local.append(pltpu.make_async_copy(upw.at[0, :, :, cols], g.at[j, :, 1], loc_sem.at[7 + 2 * j]))
     for copy in local:
         copy.start()
 
@@ -154,6 +153,17 @@
             snd.at[0, 0, slots, :, there], ms.at[sec, slots], own_send.at[d - 1, kind - 1], ms_recv.at[sec, number], where
         )
 
+    def own_across(i):
+        slot = pl.ds(4 - zh * 4 + i, 1)
+
+        @pl.when(sec < SECTIONS - 1)
+        def _():
+            remote(snd.at[0, 0, slot, :, mine], ms.at[sec, slot], zs_send.at[sec], ms_recv.at[sec, 1], across).start()
+
+        @pl.when(sec > 0)
+        def _():
+            remote(rcv.at[0, 0, slot, :, mine], mr.at[sec, slot], zr_send.at[sec], mr_recv.at[sec, 1], across).start()
+
     def aux_copies(d):
         t2 = (sec + d) % 8
         where = {"section": t2}
@@ -185,6 +195,13 @@
                 action(copy)
 
     y_weights(lambda copy: copy.start())
+    plain = gains[...].astype(F32)
+    for j in range(4):
+        rows = [
+            plain[l : l + 1, j * SHARD + b * 128 : j * SHARD + b * 128 + 128] for l in range(2) for b in range(BLOCKS)
+        ]
+        all_wide[j] = jnp.concatenate(rows + [jnp.ones((4, 128), F32)], axis=0)
+        all_gains[j] = all_wide[j].astype(BF16)
     for copy in local:
         copy.wait()
 
@@ -203,7 +220,7 @@
     up_sum = jnp.zeros((RANK, 16), F32)
     whole = jnp.zeros((16, 3 * RANK), F32)
     for j in range(4):
-        fold(g.at[j], all_gains.at[j], rw.at[0])
+        fold(g.at[j], all_wide.at[j], rw.at[0])
         here_sums = dot_nt(ones, rw[0])
         whole = whole + here_sums
         px_own[2 * j : 2 * j + 1, :] = here_sums[:1, : 2 * RANK]
@@ -219,6 +236,18 @@
     y_aux(lambda copy: copy.start())
     y_memories(lambda copy: copy.start())
 
+    slice_at = SUB * (xx * 2 + co)
+    block_at = jnp.minimum(slice_at // 128, BLOCKS - 3)
+    turn = (384 - (slice_at - block_at * 128)) % 384
+    for l in range(2):
+        window = g[zl, l, 0, :, pl.ds(pl.multiple_of(block_at * 128, 128), 384)].astype(F32)
+        own_down[l] = pltpu.roll(window, turn, 1)[:, :256]
+    own_gain = []
+    for l in range(2):
+        rows = [all_wide[zl, pl.ds(l * BLOCKS + block_at + i, 1), :] for i in range(3)]
+        rows = jnp.broadcast_to(jnp.concatenate(rows, axis=-1), (8, 384))
+        own_gain.append(pltpu.roll(rows, turn, 1)[:1, :256])
+
     for i in range(4):
         slot = zh * 4 + i
         place = jnp.int32(0)
@@ -233,8 +262,15 @@
     def w2_copy(t, d):
         return remote(w_part(t, xx), w_part(t, xx), w2_send.at[t, d - 1], w2_recv.at[t, xx], x_peer(d))
 
-    def zw_copy(t):
-        return remote(w_part(t, xx), w_part(t, xx), zw_send.at[t], w1_recv.at[t], across)
+    def zw_copy(t, piece):
+        part = w.at[t, w_layer, w_kind, half, pl.ds(piece * (SHARD // 2), SHARD // 2)]
+        return remote(part, part, zw_send.at[t, piece], wz_recv.at[t, piece], z_peer(7 if piece else 1))
+
+    def zw_sends(t, piece):
+        near = t % 2 == zh
+        if piece:
+            return jnp.logical_or(jnp.logical_and(near, zl == 0), jnp.logical_and(jnp.logical_not(near), zl > 0))
+        return jnp.logical_or(jnp.logical_and(near, zl == 3), jnp.logical_and(jnp.logical_not(near), zl < 3))
 
     def zs_copy(t):
         return remote(ms.at[t, far_slots], ms.at[t, far_slots], zs_send.at[t], ms_recv.at[t, 1], across)
@@ -257,30 +293,45 @@
             remote(mr.at[t, slots], mr.at[t, slots], zr_send.at[t], mr_recv.at[t, number], sibling).wait_recv()
 
     def relay(b):
-        @pl.when(b % 2 == zh)
+        @pl.when(jnp.logical_and(b % 2 == zh, b != sec))
         def _():
             ms_wait(b, 0)
             zs_copy(b).start()
 
-        @pl.when(b % 2 != zh)
+        @pl.when(jnp.logical_and(b % 2 != zh, b + 1 != sec))
         def _():
             mr_wait(b + 1, 0)
             zr_copy(b + 1).start()
 
+    def along_z(t, piece):
+        pl.when(zw_sends(t, piece))(lambda: zw_copy(t, piece).start())
+
     def over_x(t):
+        for d in range(1, 4):
+            w2_copy(t, d).start()
+
+    def near_weights(i, carry):
+        t = 2 * i + zh
+
         @pl.when(t != sec)
         def _():
             remote(w_part(t, xx), w_part(t, xx), own_send.at[0, 0], w1_recv.at[t], sibling).wait_recv()
 
-        pl.when(t % 2 == zh)(lambda: zw_copy(t).start())
-
-        @pl.when(t != sec)
-        def _():
-            for d in range(1, 4):
-                w2_copy(t, d).start()
-
-    def over_x_from_far(t):
-        pl.when(t % 2 != zh)(lambda: over_x(t))
+        along_z(t, 0)
+        along_z(t, 1)
+        pl.when(t != sec)(lambda: over_x(t))
+        return carry
+
+    def far_weights(piece, early):
+        def take(i, carry):
+            t = 2 * i + 1 - zh
+            zw_copy(t, piece).wait_recv()
+            along_z(t, piece)
+            if not early:
+                over_x(t)
+            return carry
+
+        lax.fori_loop(0, 4, take, 0)
 
     def w3_copy(t):
         return remote(w.at[t, :, :, half], w.at[t, :, :, half], w3_send.at[t], w3_recv.at[t], sibling)
@@ -339,18 +390,28 @@
             for n, held in enumerate((ax, px, pv)):
                 remote(held.at[t], held.at[t], ax_send.at[0, n], ax_recv.at[t, n], sibling).wait_recv()
 
-        fold(w.at[t], ax.at[t], rw.at[t % 2])
-
-    def first(i, carry):
-        over_x(2 * i + zh)
-        pl.when(i > 0)(lambda: relay(2 * i - 1))
-        relay(2 * i)
+        ax_wide[t] = ax[t].astype(F32)
+        fold(w.at[t], ax_wide.at[t], rw.at[t % 2])
+
+    for i in range(4):
+        own_across(i)
+    lax.fori_loop(0, 4, near_weights, 0)
+
+    @pl.when(zl < 2)
+    def _():
+        far_weights(0, True)
+        far_weights(1, False)
+
+    @pl.when(zl >= 2)
+    def _():
+        far_weights(1, True)
+        far_weights(0, False)
+
+    def relays(b, carry):
+        relay(b)
         return carry
 
-    lax.fori_loop(0, 4, first, 0)
-    over_x_from_far(0)
-    over_x_from_far(1)
-    over_x_from_far(2)
+    lax.fori_loop(0, SECTIONS - 1, relays, 0)
     pass_to_core(0)
     pass_to_core(1)
     ready(0)
@@ -385,7 +446,6 @@
         pl.when(t > 1)(lambda: exchange_sent(ahead, par))
         exchange_start(ahead, par, jnp.concatenate([part, packed], axis=-1).astype(BF16))
 
-        pl.when(t < SECTIONS - 3)(lambda: over_x_from_far(t + 3))
         pl.when(t < SECTIONS - 2)(lambda: pass_to_core(t + 2))
         pl.when(t < SECTIONS - 1)(lambda: ready(t + 1))
 
@@ -484,7 +544,7 @@
                 pieces = []
                 for b in (2 * n, 2 * n + 1):
                     part = xs[at, :, b * 128 : (b + 1) * 128].astype(F32)
-                    pieces.append((part - stat[at, 0]) * stat[at, 1] * gain_blocks(ax.at[t], l, b, 1))
+                    pieces.append((part - stat[at, 0]) * stat[at, 1] * gain_blocks(ax_wide.at[t], l, b, 1))
                 normed = jnp.concatenate(pieces, axis=-1).astype(BF16)
                 g[t, l, 0, :, cols] = dot_tn(dpre_s[l], normed).astype(BF16)
             g[t, 0, 1, :, cols] = dot_tn(hidden, dy0[:, cols]).astype(BF16)
@@ -516,7 +576,7 @@
                 cols = slice(n * 256 + b * 128, n * 256 + b * 128 + 128)
                 dn = moved[:, b * 128 : b * 128 + 128].astype(BF16).astype(F32)
                 hat = (xs[2 * t + 1, :, cols].astype(F32) - mean1) * rstd1
-                step = rstd1 * (dn * gain_blocks(ax.at[t], 1, 2 * n + b, 1) - one1 - hat * two1)
+                step = rstd1 * (dn * gain_blocks(ax_wide.at[t], 1, 2 * n + b, 1) - one1 - hat * two1)
                 dy0[:, cols] = (dy[:, cols].astype(F32) + step).astype(BF16)
 
         @pl.when(t > 0)
@@ -529,7 +589,7 @@
                     cols = slice(n * 256 + b * 128, n * 256 + b * 128 + 128)
                     dn = moved[:, b * 128 : b * 128 + 128].astype(BF16).astype(F32)
                     hat = (xs[2 * t, :, cols].astype(F32) - mean0) * rstd0
-                    step = rstd0 * (dn * gain_blocks(ax.at[t], 0, 2 * n + b, 1) - one0 - hat * two0)
+                    step = rstd0 * (dn * gain_blocks(ax_wide.at[t], 0, 2 * n + b, 1) - one0 - hat * two0)
                     out = (dy0[:, cols].astype(F32) + step).astype(BF16).astype(F32)
                     dy[:, cols] = scaled_value(out).astype(BF16)
 
@@ -546,7 +606,7 @@
         r0_copy(t).wait_recv()
         for l in range(2):
             for kind in range(2):
-                hs[t, l, kind] = (g[t, l, kind, half, :].astype(F32) + cr[t, l, kind].astype(F32)).astype(BF16)
+                hs[t, l, kind] = g[t, l, kind, half, :] + cr[t, l, kind]
         for d in range(1, 4):
             r1_copy(t, d).start()
 
@@ -605,13 +665,13 @@
             gradients(t + 1)
             r0_copy(t + 1).start()
 
-        pl.when(within(2))(lambda: r1_start(t + 2))
         pl.when(within(3))(lambda: r2_start(t + 3))
-        pl.when(within(4))(lambda: r3_start(t + 4))
+        pl.when(within(5))(lambda: r3_start(t + 5))
         pl.when(k < SECTIONS)(lambda: finish(t, par))
+        pl.when(within(1))(lambda: r1_start(t + 1))
         return carry
 
-    lax.fori_loop(0, SECTIONS + 4, backward, 0)
+    lax.fori_loop(0, SECTIONS + 5, backward, 0)
 
     for q in range(8):
         source_rep = (source_z % 4) * 8 + q
@@ -626,6 +686,12 @@
             rows = slice(part * 32, (part + 1) * 32)
             out_d[l, rows, :] = orr[l * 4 + part][:, :SUB]
             out_u[l, rows, :] = orr[l * 4 + 2 + part][:, :SUB]
+        along = jnp.zeros((1, 256), F32)
+        for part in range(2):
+            along = along + jnp.sum(
+                own_down[l, part * 32 : part * 32 + 32, :] * orr[l * 4 + part].astype(F32), axis=0, keepdims=True
+            )
+        out_g[l : l + 1, :] = (along / own_gain[l])[:, :SUB]
 
     y_weights(lambda copy: copy.wait_send())
     y_aux(lambda copy: copy.wait_send())
@@ -634,10 +700,11 @@
     exchange_sent(back, 1)
 
     def drain(t, carry):
+        for piece in range(2):
+            pl.when(zw_sends(t, piece))(functools.partial(lambda piece: zw_copy(t, piece).wait_send(), piece))
+
         @pl.when(t % 2 == zh)
         def _():
-            zw_copy(t).wait_send()
-
             @pl.when(t < SECTIONS - 1)
             def _():
                 zs_copy(t).wait_send()
@@ -669,31 +736,31 @@
 
 def local(inputs, cotangent, send_memory, recv_memory, sample_ids, gains, down_weight, up_weight):
     dwt = jnp.swapaxes(down_weight, 2, 3)
-    gain = gains[0].astype(F32)
-    rows = jnp.swapaxes(gain.reshape(2, 4, BLOCKS, 128), 0, 1).reshape(4, 2 * BLOCKS, 128)
-    rows = jnp.pad(rows, ((0, 0), (0, 4), (0, 0)))
-
     anywhere = pl.BlockSpec(memory_space=pl.ANY)
     vmem = pl.BlockSpec(memory_space=pltpu.VMEM)
     sem = pltpu.SemaphoreType.DMA
-    grad_down, grad_up = pl.pallas_call(
+    grad_down, grad_up, grad_gain = pl.pallas_call(
         kernel,
         out_shape=(
             jax.ShapeDtypeStruct((2, RANK, SUB), BF16),
             jax.ShapeDtypeStruct((2, RANK, SUB), BF16),
+            jax.ShapeDtypeStruct((2, SUB), F32),
         ),
-        in_specs=[pl.BlockSpec(memory_space=pltpu.SMEM)] + [anywhere] * 7,
-        out_specs=(vmem, vmem),
+        in_specs=[pl.BlockSpec(memory_space=pltpu.SMEM)] + [anywhere] * 6 + [vmem],
+        out_specs=(vmem, vmem, vmem),
         scratch_shapes=[
             pltpu.VMEM((8, 2, 2, RANK, SHARD), BF16),
             pltpu.VMEM((8, 8, 16, SHARD), BF16),
             pltpu.VMEM((8, 8, 16, SHARD), BF16),
-            pltpu.VMEM((8, 32, 128), F32),
+            pltpu.VMEM((8, 32, 128), BF16),
             pltpu.VMEM((8, 8, 128), F32),
             pltpu.VMEM((8, RANK, 128), BF16),
             pltpu.VMEM((8, 128), F32),
             pltpu.VMEM((RANK, 128), BF16),
+            pltpu.VMEM((4, 32, 128), BF16),
             pltpu.VMEM((4, 32, 128), F32),
+            pltpu.VMEM((8, 32, 128), F32),
+            pltpu.VMEM((2, RANK, 256), F32),
             pltpu.VMEM((2, 3 * RANK, SHARD), BF16),
             pltpu.VMEM((16, TOKENS, SHARD), BF16),
             pltpu.VMEM((TOKENS, SHARD), BF16),
@@ -717,14 +784,15 @@
             pltpu.VMEM((8, 7, 32, 256), BF16),
             pltpu.VMEM((8, 32, 256), BF16),
             pltpu.VMEM((8, 32, 256), BF16),
-            sem((15,)),
+            sem((14,)),
             sem((3, 5)),
             sem((7, 3)),
             sem((8,)),
+            sem((8, 2)),
             sem((8, 3)),
             sem((8, 2)),
             sem((8, 2)),
-            sem((8,)),
+            sem((8, 2)),
             sem((8,)),
             sem((8,)),
             sem((8, 3)),
@@ -748,12 +816,8 @@
             collective_id=0, has_side_effects=True, vmem_limit_bytes=56 * 1024 * 1024
         ),
         name="relay",
-    )(sample_ids, inputs, cotangent, send_memory, recv_memory, dwt, up_weight, rows)
-
-    start = lax.axis_index("dp") * SUB
-    own_down = lax.dynamic_slice_in_dim(dwt[0], start, SUB, 2).astype(F32)
-    own_gain = lax.dynamic_slice_in_dim(gain, start, SUB, 1)
-    grad_gain = jnp.sum(own_down * grad_down.astype(F32), axis=1) / own_gain
+    )(sample_ids, inputs, cotangent, send_memory, recv_memory, dwt, up_weight, gains[0])
+
     return (
         jnp.swapaxes(grad_down, 1, 2)[None],
         grad_up[None],

time: 214 us -> 206 us (0.963); the launches traced: 213 us -> 203 us
  Pallas kernels: 206 us -> 198 us
    pallas_call x1, Pallas kernels: 206 us -> 198 us  [local(): pl.pallas_call(kernel, out_shape=(jax.ShapeDtypeStruct((2, RANK, SUB), BF...]
where the time goes in v3:
time: 206 us; the launch traced here: 203 us
  Pallas kernels  198 us (96%)
  local copies, waits for them, and re-layouts  2.94 us (1%)
    pallas_call x1, Pallas kernels, local(): pl.pallas_call(kernel, out_shape=(jax.ShapeDtypeStruct((2, RANK, SUB), BF...  198 us

profile of v3, /device:TPU:4, one launch (start us, length us, event | category | flops | bytes accessed | tf_op | source)
XLA Modules:
  0.0 202.9 jit_solution(11244513613324105189)
XLA Ops:
  0.6 198.1 %relay.1 = (bf16[2,64,224]{2,1,0:T(8,128)(2,1)}, bf16[2,64,224]{2,1,0:T(8,128)(2,1)}, f32[2,224]{1,0:T(2,128)}) custom-call(s32[1,8]{1,0:T(1,128)} %ids.1, bf16[1,8,16,7168]{3,2,1,0:T(8,128)(2,1)} %inp.1, bf16[1,8,16,7168]{3,2,1,0:T(8,128)(2,1)} %cot.1, bf16[1,1,8,16,7168]{4,3,2,1,0:T(8,128)(2,1)} %snd.1, bf16[1,1,8,16,7168]{4,3,2,1,0:T(8,128)(2,1)} %rcv.1, ...), custom_call_target="tpu_custom_call" | custom-call | tf_op jit(solution)/shard_map/relay/pallas_call | solution.py:742
  198.7 1.2 convert_bitcast_fusion
  199.9 1.5 copy.13
  201.4 1.5 copy.14

commit v4 on v3

--- a/solution.py
+++ b/solution.py
@@ -101,7 +101,7 @@
         cols = slice(j * SHARD, (j + 1) * SHARD)
         local.append(pltpu.make_async_copy(dwt.at[0, :, :, cols], g.at[j, :, 0], loc_sem.at[6 + 2 * j]))
         local.append(pltpu.make_async_copy(upw.at[0, :, :, cols], g.at[j, :, 1], loc_sem.at[7 + 2 * j]))
-    for copy in local:
+    for copy in local[6:] + local[:6]:
         copy.start()
 
     barrier = pltpu.get_barrier_semaphore()
@@ -195,6 +195,8 @@
                 action(copy)
 
     y_weights(lambda copy: copy.start())
+    for i in range(4):
+        own_across(i)
     plain = gains[...].astype(F32)
     for j in range(4):
         rows = [
@@ -202,7 +204,7 @@
         ]
         all_wide[j] = jnp.concatenate(rows + [jnp.ones((4, 128), F32)], axis=0)
         all_gains[j] = all_wide[j].astype(BF16)
-    for copy in local:
+    for copy in local[6:]:
         copy.wait()
 
     def gain_blocks(rows_ref, l, first, count):
@@ -235,6 +237,8 @@
     pv[sec] = pv_own[...]
     y_aux(lambda copy: copy.start())
     y_memories(lambda copy: copy.start())
+    for copy in local[:6]:
+        copy.wait()
 
     slice_at = SUB * (xx * 2 + co)
     block_at = jnp.minimum(slice_at // 128, BLOCKS - 3)
@@ -393,8 +397,6 @@
         ax_wide[t] = ax[t].astype(F32)
         fold(w.at[t], ax_wide.at[t], rw.at[t % 2])
 
-    for i in range(4):
-        own_across(i)
     lax.fori_loop(0, 4, near_weights, 0)
 
     @pl.when(zl < 2)
@@ -415,6 +417,10 @@
     pass_to_core(0)
     pass_to_core(1)
     ready(0)
+
+    def send_back(t, par):
+        part = dot_nt(dy[...], w[t, :, 1].reshape(2 * RANK, SHARD))
+        exchange_start(back, par, part.astype(BF16))
 
     def wide(column):
         return jnp.broadcast_to(column, (TOKENS, 128))
@@ -446,6 +452,7 @@
         pl.when(t > 1)(lambda: exchange_sent(ahead, par))
         exchange_start(ahead, par, jnp.concatenate([part, packed], axis=-1).astype(BF16))
 
+        pl.when(t == SECTIONS - 1)(lambda: send_back(t, 0))
         pl.when(t < SECTIONS - 2)(lambda: pass_to_core(t + 2))
         pl.when(t < SECTIONS - 1)(lambda: ready(t + 1))
 
@@ -525,9 +532,11 @@
     exchange_sent(ahead, 1)
 
     def begin(t, par):
-        part = dot_nt(dy[...], w[t, :, 1].reshape(2 * RANK, SHARD))
-        pl.when(t < SECTIONS - 2)(lambda: exchange_sent(back, par))
-        exchange_start(back, par, part.astype(BF16))
+        @pl.when(t < SECTIONS - 1)
+        def _():
+            pl.when(t < SECTIONS - 2)(lambda: exchange_sent(back, par))
+            send_back(t, par)
+
         gp_s[0] = gelu_slope(pre_s[2 * t])
         gp_s[1] = gelu_slope(pre_s[2 * t + 1])
         hidden = hid_s[2 * t + 1]

time: 206 us -> 201 us (0.976)
  Pallas kernels: 198 us -> 193 us
    pallas_call x1, Pallas kernels: 198 us -> 193 us  [local(): pl.pallas_call(kernel, out_shape=(jax.ShapeDtypeStruct((2, RANK, SUB), BF...]
where the time goes in v4:
time: 201 us; the launch traced here: 198 us
  Pallas kernels  193 us (96%)
  local copies, waits for them, and re-layouts  2.94 us (1%)
    pallas_call x1, Pallas kernels, local(): pl.pallas_call(kernel, out_shape=(jax.ShapeDtypeStruct((2, RANK, SUB), BF...  193 us

profile of v4, /device:TPU:4, one launch (start us, length us, event | category | flops | bytes accessed | tf_op | source)
XLA Modules:
  0.0 197.6 jit_solution(2456561412321373811)
XLA Ops:
  0.6 192.7 %relay.1 = (bf16[2,64,224]{2,1,0:T(8,128)(2,1)}, bf16[2,64,224]{2,1,0:T(8,128)(2,1)}, f32[2,224]{1,0:T(2,128)}) custom-call(s32[1,8]{1,0:T(1,128)} %ids.1, bf16[1,8,16,7168]{3,2,1,0:T(8,128)(2,1)} %inp.1, bf16[1,8,16,7168]{3,2,1,0:T(8,128)(2,1)} %cot.1, bf16[1,1,8,16,7168]{4,3,2,1,0:T(8,128)(2,1)} %snd.1, bf16[1,1,8,16,7168]{4,3,2,1,0:T(8,128)(2,1)} %rcv.1, ...), custom_call_target="tpu_custom_call" | custom-call | tf_op jit(solution)/shard_map/relay/pallas_call | solution.py:751
  193.4 1.2 convert_bitcast_fusion
  194.6 1.5 copy.13
  196.1 1.5 copy.14
